TPU v7x, 256 devices: a whole 4x4x8 slice. The times are simulated.
256 devices in a mesh: kz: 16 (over z_lo, x, core), freq: 16 (over z_hi, y).
Axes of the slice: x: 4, y: 4, z: 8 (z_hi: 4, z_lo: 2; z = z_hi * 2 + z_lo), core: 2. Of those that a mesh axis runs over, the one named last changes fastest.
Arguments:
- green: float32 [1, 2, 512, 32, 1024], P(None, None, 'freq', 'kz'), may hold values from -6 to 6
- interaction: float32 [1, 2, 256, 32, 1024], P(None, None, 'freq', 'kz'), may hold values from -6 to 6
Outputs:
- self_energy: float32 [2, 512, 32, 1024], P(None, 'freq', 'kz')
- bubble: float32 [1, 2, 256, 32, 1024], P(None, None, 'freq', 'kz')
All inputs are finite; a program needn't handle non-finite values.
Results may differ from a plain program's by a relative error of at most 0.000098.
Values sent between devices are 32-bit elements; how exact they have to be, the bound alone decides.
A program may use at most 64 MiB of HBM per device.

v0:
```python
import functools
import math

import jax
import jax.numpy as jnp
import ml_dtypes
import numpy as np
from jax import lax
from jax.experimental import pallas as pl
from jax.experimental.pallas import tpu as pltpu
from jax.sharding import PartitionSpec as P

MESH = pl.DeviceIdType.MESH
F32 = jnp.float32
BF16 = jnp.bfloat16


def split_table(table):
    high = table.astype(ml_dtypes.bfloat16)
    low = (table - high.astype(np.float64)).astype(ml_dtypes.bfloat16)
    return np.stack([high, low])


def y_sets():
    sets = [[0, 16, 8, 24]]
    singles = [v for v in range(1, 16) if v != 8]
    for k in range(7):
        a, b = singles[2 * k], singles[2 * k + 1]
        sets.append([a, 32 - a, b, 32 - b])
    return sets


def columns(residue):
    if residue == 0:
        xs = [[0, 8], [16, 24]]
    elif residue == 4:
        xs = [[4, 12], [28, 20]]
    elif residue < 4:
        m = residue
        xs = [[m, m + 8], [m + 16, m + 24]]
    else:
        m = 8 - residue
        xs = [[16 - m, 8 - m], [32 - m, 24 - m]]
    sets = y_sets()
    x = np.zeros(128, np.int64)
    y = np.zeros(128, np.int64)
    for pair in range(2):
        for k in range(8):
            for half in range(2):
                for i in range(4):
                    lane = pair * 64 + k * 8 + half * 4 + i
                    x[lane] = xs[half][pair]
                    y[lane] = sets[k][i]
    return x, y


def real_form(angle, scale):
    c, s = np.cos(angle) * scale, np.sin(angle) * scale
    return np.block([[c, s], [-s, c]])


def sheet_tables():
    tables = []
    xl = np.repeat(np.arange(4), 32)
    ky = np.tile(np.arange(32), 4)
    for residue in range(8):
        x, y = columns(residue)
        angle = 2 * np.pi * ((xl[:, None] * x + ky[:, None] * y) % 32) / 32
        tables.append(real_form(angle, 1 / 32))
    return np.stack(tables)


def depth_tables():
    whole, parts = [], []
    kappa = np.arange(16)
    for parity in range(2):
        depth = 2 * np.arange(16) + parity
        angle = 2 * np.pi * ((depth[:, None] * kappa) % 32) / 32
        c, s = np.cos(angle) / math.sqrt(32), np.sin(angle) / math.sqrt(32)
        eye = np.eye(8)
        whole.append(np.block([[np.kron(c, eye), np.kron(-s, eye)], [np.kron(s, eye), np.kron(c, eye)]]))
        parts.append(np.concatenate([np.kron(c, eye), np.kron(s, eye)], 0))
    return np.stack(whole), np.stack(parts)


def angles(length, offset):
    p = 2 * np.arange(length) - length + offset
    j = np.arange(256)
    return 2 * np.pi * ((p[:, None] * (2 * j + 1)) % 2048) / 2048


def fermi_table():
    theta = angles(512, 1).reshape(4, 4, 32, 256).transpose(1, 0, 2, 3).reshape(512, 256)
    return np.concatenate([np.cos(theta), np.sin(theta)], 1) / math.sqrt(512)


def bose_tables():
    theta = angles(256, 0).reshape(4, 4, 16, 256).transpose(1, 0, 2, 3)
    c, s = np.cos(theta), np.sin(theta)
    real = np.concatenate([c, -s, c, s], -1)
    imag = np.concatenate([s, c, -s, c], -1)
    there = np.stack([real, imag], 1).reshape(512, 1024) / math.sqrt(256)
    zero = np.zeros_like(c)
    real = np.concatenate([c, zero, zero, -s], -1)
    imag = np.concatenate([zero, c, s, zero], -1)
    back = np.stack([real, imag], 1).reshape(512, 1024).T / math.sqrt(512)
    return there, back


def mirror_tables():
    tables = np.zeros((8, 128, 128))
    for parity in range(2):
        for self_x in range(2):
            for self_y in range(2):
                for depth in range(16):
                    other = (-depth - parity) % 16
                    for half in range(2):
                        for i in range(4):
                            h = half if self_x else 1 - half
                            n = [0, 1, 3, 2][i] if self_y else [1, 0, 3, 2][i]
                            row = depth * 8 + half * 4 + i
                            tables[parity * 4 + self_x * 2 + self_y, row, other * 8 + h * 4 + n] = 1
    return tables.astype(ml_dtypes.bfloat16)


@functools.cache
def tables():
    sheet = sheet_tables()
    whole, parts = depth_tables()
    fermi = fermi_table()
    there, back = bose_tables()
    parts_back = np.concatenate(
        [parts[:, :128].transpose(0, 2, 1), parts[:, 128:].transpose(0, 2, 1)], 1
    )
    return (
        split_table(sheet),
        split_table(sheet.transpose(0, 2, 1)),
        np.ascontiguousarray(split_table(whole).swapaxes(0, 1)),
        np.ascontiguousarray(split_table(whole.transpose(0, 2, 1)).swapaxes(0, 1)),
        np.ascontiguousarray(split_table(parts).swapaxes(0, 1)),
        np.ascontiguousarray(split_table(parts_back).swapaxes(0, 1)),
        split_table(fermi),
        split_table(fermi.T),
        split_table(there),
        split_table(back),
        mirror_tables(),
    )


def split(x):
    high = x.astype(BF16)
    return high, (x - high.astype(F32)).astype(BF16)


def dot(a, b):
    return jnp.dot(a, b, preferred_element_type=F32)


def data_by_table(x, table):
    high, low = split(x)
    return dot(high, table[0]) + dot(low, table[0]) + dot(high, table[1])


def table_by_data(table, x):
    high, low = split(x)
    return dot(table[0], high) + dot(table[0], low) + dot(table[1], high)


def four(re, im, sign):
    s0r, s0i = re[0] + re[2], im[0] + im[2]
    d0r, d0i = re[0] - re[2], im[0] - im[2]
    s1r, s1i = re[1] + re[3], im[1] + im[3]
    d1r, d1i = re[1] - re[3], im[1] - im[3]
    tr, ti = (-d1i, d1r) if sign > 0 else (d1i, -d1r)
    return [s0r + s1r, d0r + tr, s0r - s1r, d0r - tr], [s0i + s1i, d0i + ti, s0i - s1i, d0i - ti]


def eight(re, im, sign):
    er, ei = four(re[0::2], im[0::2], sign)
    orr, oi = four(re[1::2], im[1::2], sign)
    h = math.sqrt(0.5)
    tr = [orr[0]]
    ti = [oi[0]]
    if sign > 0:
        tr += [h * (orr[1] - oi[1]), -oi[2], -h * (orr[3] + oi[3])]
        ti += [h * (orr[1] + oi[1]), orr[2], h * (orr[3] - oi[3])]
    else:
        tr += [h * (orr[1] + oi[1]), oi[2], h * (oi[3] - orr[3])]
        ti += [h * (oi[1] - orr[1]), -orr[2], -h * (orr[3] + oi[3])]
    return (
        [er[k] + tr[k] for k in range(4)] + [er[k] - tr[k] for k in range(4)],
        [ei[k] + ti[k] for k in range(4)] + [ei[k] - ti[k] for k in range(4)],
    )


PAIRS = ((1, 7, 2), (2, 6, 4), (3, 5, 6))


def sheet_there(x, table, out):
    rows = x.shape[1]
    re = [x[0, :, 128 * g : 128 * g + 128] for g in range(8)]
    im = [x[1, :, 128 * g : 128 * g + 128] for g in range(8)]
    yr, yi = eight(re, im, 1)
    first = lax.broadcasted_iota(jnp.int32, (rows, 256), 1) % 8 < 4

    def one(residue):
        both = jnp.concatenate([yr[residue], yi[residue]], 1)
        return data_by_table(both, (table[0, residue], table[1, residue]))

    def put(group, value):
        out[group, 0] = value[:, :128]
        out[group, 1] = value[:, 128:]

    put(0, one(0))
    put(1, one(4))
    for m, n, group in PAIRS:
        a, b = one(m), one(n)
        put(group, jnp.where(first, a, b))
        put(group + 1, jnp.where(first, b, a))


def sheet_back(x, table, out):
    rows = x.shape[2]
    first = lax.broadcasted_iota(jnp.int32, (rows, 256), 1) % 8 < 4
    held = [None] * 8

    def get(group):
        return jnp.concatenate([x[group, 0], x[group, 1]], 1)

    held[0], held[4] = get(0), get(1)
    for m, n, group in PAIRS:
        a, b = get(group), get(group + 1)
        held[m] = jnp.where(first, a, b)
        held[n] = jnp.where(first, b, a)
    re, im = [], []
    for residue in range(8):
        y = data_by_table(held[residue], (table[0, residue], table[1, residue]))
        re.append(y[:, :128])
        im.append(y[:, 128:])
    re, im = eight(re, im, -1)
    for g in range(8):
        out[0, :, 128 * g : 128 * g + 128] = re[g]
        out[1, :, 128 * g : 128 * g + 128] = im[g]


def swap_parts(x, sign):
    rows = x.shape[0]
    lower = lax.broadcasted_iota(jnp.int32, (rows, 128), 1) < 64
    pieces = []
    for y in range(4):
        turned = pltpu.roll(x[:, 128 * y : 128 * y + 128], 64, 1)
        pieces.append(jnp.where(lower, -turned, turned) if sign > 0 else jnp.where(lower, turned, -turned))
    return jnp.concatenate(pieces, 1)


def kernel(
    green, inter, sheet_h, sheetb_h, whole_h, wholeb_h, parts_h, partsb_h, fermi_h, fermib_h, bose_h, boseb_h, mirror_h,
    out_g, out_v,
    x_g, x_v, sheet, sheetb, whole, wholeb, parts, partsb, fermi, fermib, bose, boseb, mirror,
    sa_g, sa_v, ra_g, ra_v, sb_g, sb_v, rb_g, rb_v, g_time,
    tb_g, tb_v, ub_g, ub_v, ta_g, ta_v, ua_g, ua_v, y_g, y_v,
    load_sem, sem,
):
    kz, freq = lax.axis_index("kz"), lax.axis_index("freq")
    z_lo, c = kz // 8, kz % 8
    z_hi, y = freq // 4, freq % 4
    z = z_hi * 2 + z_lo
    o = c * 4 + y
    parity = o // 16
    self_x = jnp.where(jnp.logical_and(z == 0, (o % 16) // 8 == 0), 1, 0)
    self_y = jnp.where(o % 8 == 0, 1, 0)

    loads = {}
    for k, (name, src, dst) in enumerate(
        [
            ("x_g", green, x_g),
            ("sheet", sheet_h, sheet),
            ("x_v", inter, x_v),
            ("whole", whole_h.at[parity], whole),
            ("fermi", fermi_h, fermi),
            ("mirror", mirror_h.at[parity * 4 + self_x * 2 + self_y], mirror),
            ("boseb", boseb_h, boseb),
            ("partsb", partsb_h.at[parity], partsb),
            ("parts", parts_h.at[parity], parts),
            ("bose", bose_h, bose),
            ("fermib", fermib_h, fermib),
            ("wholeb", wholeb_h.at[parity], wholeb),
            ("sheetb", sheetb_h, sheetb),
        ]
    ):
        loads[name] = pltpu.make_async_copy(src, dst, load_sem.at[k])
        loads[name].start()

    def z_peer(d):
        other = (z + d) % 8
        return other, {"kz": (other % 2) * 8 + c, "freq": (other // 2) * 4 + y}

    def o_peer(d):
        other = (o + d) % 32
        return other, {"kz": z_lo * 8 + other // 4, "freq": z_hi * 4 + other % 4}

    barrier = pltpu.get_barrier_semaphore()
    for d in range(1, 8):
        pl.semaphore_signal(barrier, inc=1, device_id=z_peer(d)[1], device_id_type=MESH)

    def greet(d, carry):
        pl.semaphore_signal(barrier, inc=1, device_id=o_peer(d)[1], device_id_type=MESH)
        return carry

    lax.fori_loop(1, 32, greet, 0)

    count = [0]

    def new_sem():
        count[0] += 1
        return sem.at[count[0] - 1]

    sent = []

    def exchange_z(src, dst):
        s, r, l = new_sem(), new_sem(), new_sem()
        own = pltpu.make_async_copy(src.at[z], dst.at[z], l)
        for d in (1, 7, 2, 6, 3, 5, 4):
            other, device = z_peer(d)
            pltpu.make_async_remote_copy(
                src.at[other], dst.at[z], s, r, device_id=device, device_id_type=MESH
            ).start()
        own.start()
        seven = pltpu.make_async_remote_copy(
            src.at[pl.ds(0, 7)], dst.at[pl.ds(0, 7)], s, r, device_id=z_peer(1)[1], device_id_type=MESH
        )
        sent.append(seven)

        def wait():
            seven.wait_recv()
            own.wait()

        return wait

    def exchange_o(src_at, dst_at, src_31, dst_31):
        s, r, l = new_sem(), new_sem(), new_sem()
        own = pltpu.make_async_copy(src_at(o), dst_at(o), l)

        def send(d, carry):
            other, device = o_peer(d)
            pltpu.make_async_remote_copy(
                src_at(other), dst_at(o), s, r, device_id=device, device_id_type=MESH
            ).start()
            return carry

        lax.fori_loop(1, 32, send, 0)
        own.start()
        rest = pltpu.make_async_remote_copy(
            src_31, dst_31, s, r, device_id=o_peer(1)[1], device_id_type=MESH
        )
        sent.append(rest)

        def wait():
            rest.wait_recv()
            own.wait()

        return wait

    def rows_at(ref):
        def at(k):
            piece = pl.ds(pl.multiple_of(k * 8, 8), 8)
            return ref.at[:, :, piece, :] if len(ref.shape) == 4 else ref.at[:, piece, :]

        return at

    def planes_at(ref):
        def at(k):
            planes = pl.ds(2 * (k // 4), 2)
            lanes = pl.ds(pl.multiple_of((k % 4) * 128, 128), 128)
            return ref.at[:, planes, :, lanes] if len(ref.shape) == 4 else ref.at[planes, :, lanes]

        return at

    def rows_31(ref):
        return ref.at[:, :, pl.ds(0, 248), :] if len(ref.shape) == 4 else ref.at[:, pl.ds(0, 248), :]

    loads["x_g"].wait()
    loads["sheet"].wait()
    sheet_there(x_g, sheet, sa_g)
    pl.semaphore_wait(barrier, 38)
    a_g = exchange_z(sa_g, ra_g)
    loads["x_v"].wait()
    sheet_there(x_v, sheet, sa_v)
    a_v = exchange_z(sa_v, ra_v)

    a_g()
    for p in range(2):
        for b in range(2):
            even = jnp.concatenate([ra_g[2 * h, p, pl.ds(b, 32, 2), :] for h in range(4)], 0)
            odd = jnp.concatenate([ra_g[2 * h + 1, p, pl.ds(b, 32, 2), :] for h in range(4)], 0)
            sb_g[p, b, :128, :] = (even + odd).T
            sb_g[p, b, 128:, :] = (even - odd).T
    b_g = exchange_o(rows_at(sb_g), planes_at(rb_g), rows_31(sb_g), rows_31(ub_g))
    a_v()
    for b in range(2):
        even = jnp.concatenate(
            [ra_v[2 * h, p, pl.ds(b, 16, 2), :] for p in range(2) for h in range(4)], 0
        )
        odd = jnp.concatenate(
            [ra_v[2 * h + 1, p, pl.ds(b, 16, 2), :] for p in range(2) for h in range(4)], 0
        )
        sb_v[b, :128, :] = (even + odd).T
        sb_v[b, 128:, :] = (even - odd).T
    b_v = exchange_o(rows_at(sb_v), planes_at(rb_v), rows_31(sb_v), rows_31(ub_v))

    b_g()
    loads["whole"].wait()
    lattice = table_by_data((whole[0], whole[1]), rb_g[...].reshape(256, 512))
    loads["fermi"].wait()
    both = data_by_table(lattice, (fermi[0], fermi[1]))
    ca, sa = both[:128, :256], both[:128, 256:]
    cb, sb = both[128:, :256], both[128:, 256:]
    g_time[...] = jnp.concatenate([ca + sb, cb - sa, sb - ca, -(cb + sa)], 1)
    g1r, g1i, g2r, g2i = [g_time[:, 256 * k : 256 * k + 256] for k in range(4)]
    loads["mirror"].wait()
    high, low = split(g_time[...])
    turned = dot(mirror[...], high) + dot(mirror[...], low)
    m1r, m1i, m2r, m2i = [turned[:, 256 * k : 256 * k + 256] for k in range(4)]
    b1r, b1i = g1i * m2i - g1r * m2r, -(g1r * m2i + g1i * m2r)
    b2r, b2i = g2i * m1i - g2r * m1r, -(g2r * m1i + g2i * m1r)
    loads["boseb"].wait()
    nu = data_by_table(
        jnp.concatenate([b1r + b2r, b1i + b2i, b1r - b2r, b1i - b2i], 1), (boseb[0], boseb[1])
    )
    loads["partsb"].wait()
    cs = table_by_data((partsb[0], partsb[1]), nu)
    tb_v[...] = (cs[:128] + swap_parts(cs[128:], -1)).reshape(16, 8, 512)
    c_v = exchange_o(planes_at(tb_v), rows_at(ub_v), rows_31(sb_v), rows_31(ub_v))

    b_v()
    loads["parts"].wait()
    cs = table_by_data((parts[0], parts[1]), rb_v[...].reshape(128, 512))
    loads["bose"].wait()
    v_time = data_by_table(cs[:128] + swap_parts(cs[128:], 1), (bose[0], bose[1]))
    v1r, v1i, v2r, v2i = [v_time[:, 256 * k : 256 * k + 256] for k in range(4)]
    g1r, g1i, g2r, g2i = [g_time[:, 256 * k : 256 * k + 256] for k in range(4)]
    s1r, s1i = v1r * g1r - v1i * g1i, v1r * g1i + v1i * g1r
    s2r, s2i = v2r * g2r - v2i * g2i, v2r * g2i + v2i * g2r
    loads["fermib"].wait()
    omega = data_by_table(
        jnp.concatenate(
            [
                jnp.concatenate([s1r - s2r, -(s1i + s2i)], 1),
                jnp.concatenate([s1i - s2i, s1r + s2r], 1),
            ],
            0,
        ),
        (fermib[0], fermib[1]),
    )
    loads["wholeb"].wait()
    tb_g[...] = table_by_data((wholeb[0], wholeb[1]), omega).reshape(2, 16, 8, 512)
    c_g = exchange_o(planes_at(tb_g), rows_at(ub_g), rows_31(sb_g), rows_31(ub_g))

    c_v()
    for b in range(2):
        even, odd = ub_v[b, :128, :].T, ub_v[b, 128:, :].T
        for lo, value in ((0, even + odd), (1, even - odd)):
            for p in range(2):
                for h in range(4):
                    k = 64 * p + 16 * h
                    ta_v[2 * h + lo, p, pl.ds(b, 16, 2), :] = value[k : k + 16]
    d_v = exchange_z(ta_v, ua_v)
    c_g()
    for p in range(2):
        for b in range(2):
            even, odd = ub_g[p, b, :128, :].T, ub_g[p, b, 128:, :].T
            for lo, value in ((0, even + odd), (1, even - odd)):
                for h in range(4):
                    ta_g[2 * h + lo, p, pl.ds(b, 32, 2), :] = value[32 * h : 32 * h + 32]
    d_g = exchange_z(ta_g, ua_g)

    d_v()
    loads["sheetb"].wait()
    sheet_back(ua_v, sheetb, y_v)
    put_v = pltpu.make_async_copy(y_v, out_v, load_sem.at[13])
    put_v.start()
    d_g()
    sheet_back(ua_g, sheetb, y_g)
    put_g = pltpu.make_async_copy(y_g, out_g, load_sem.at[14])
    put_g.start()
    for copy in sent:
        copy.wait_send()
    put_v.wait()
    put_g.wait()


def per_device(green, inter):
    shapes = [
        (2, 64, 1024), (2, 32, 1024),
        (2, 8, 256, 256), (2, 8, 256, 256), (2, 256, 256), (2, 256, 256), (2, 256, 128), (2, 256, 128),
        (2, 512, 512), (2, 512, 512), (2, 512, 1024), (2, 1024, 512), (128, 128),
        (8, 2, 64, 128), (8, 2, 32, 128), (8, 2, 64, 128), (8, 2, 32, 128),
        (2, 2, 256, 128), (2, 256, 128), (2, 16, 8, 512), (16, 8, 512), (128, 1024),
        (2, 16, 8, 512), (16, 8, 512), (2, 2, 256, 128), (2, 256, 128),
        (8, 2, 64, 128), (8, 2, 32, 128), (8, 2, 64, 128), (8, 2, 32, 128), (2, 64, 1024), (2, 32, 1024),
    ]
    scratch = [pltpu.VMEM(s, BF16 if 2 <= k < 13 else F32) for k, s in enumerate(shapes)]
    any_spec = pl.BlockSpec(memory_space=pl.ANY)
    constants = tables()
    out_g, out_v = pl.pallas_call(
        kernel,
        out_shape=(
            jax.ShapeDtypeStruct((2, 64, 1024), F32),
            jax.ShapeDtypeStruct((2, 32, 1024), F32),
        ),
        in_specs=[any_spec] * (2 + len(constants)),
        out_specs=(any_spec, any_spec),
        scratch_shapes=scratch + [pltpu.SemaphoreType.DMA((15,)), pltpu.SemaphoreType.DMA((24,))],
        compiler_params=pltpu.CompilerParams(
            collective_id=0, has_side_effects=True, vmem_limit_bytes=56 << 20
        ),
    )(green.reshape(2, 64, 1024), inter.reshape(2, 32, 1024), *constants)
    return out_g.reshape(2, 32, 2, 1024), out_v.reshape(1, 2, 16, 2, 1024)


def solution(mesh):
    placed = (P(None, None, "freq", "kz", None), P(None, None, "freq", "kz", None))
    return jax.shard_map(
        per_device,
        mesh=mesh,
        in_specs=placed,
        out_specs=(P(None, "freq", "kz", None), P(None, None, "freq", "kz", None)),
        check_vma=False,
    )
```

profile of v0, /device:TPU:1, one launch (start us, length us, event | category | flops | bytes accessed | tf_op | source)
XLA Modules:
  0.0 75.3 jit_solution(4538578356290266030)
XLA Ops:
  0.6 1.8 %reshape.17.inter = f32[2,32,1024]{2,1,0:T(8,128)} reshape(f32[1,2,16,2,1024]{4,3,2,1,0:T(2,128)} %param.14) | data formatting | bytes 524288 | tf_op jit(solution)/shard_map/reshape | solution.py:517
  2.5 2.2 %reshape.16.green = f32[2,64,1024]{2,1,0:T(8,128)} reshape(f32[1,2,32,2,1024]{4,3,2,1,0:T(2,128)} %param.13) | data formatting | bytes 1048576 | tf_op jit(solution)/shard_map/reshape | solution.py:517
  4.7 66.7 %shard_map.140 = (f32[2,64,1024]{2,1,0:T(8,128)}, f32[2,32,1024]{2,1,0:T(8,128)}) custom-call(f32[2,64,1024]{2,1,0:T(8,128)} %reshape.16.green, f32[2,32,1024]{2,1,0:T(8,128)} %reshape.17.inter, bf16[2,8,256,256]{3,2,1,0:T(8,128)(2,1)} %constant.22.clone.sheet_h, bf16[2,8,256,256]{3,2,1,0:T(8,128)(2,1)} %constant.23.clone.sheetb_h, ...), custom_call_target="tpu_custom_call" | custom-call | tf_op jit(solution)/shard_map/pallas_call | solution.py:505
  71.3 2.1 %reshape.18 = f32[2,32,2,1024]{3,2,1,0:T(2,128)} reshape(f32[2,64,1024]{2,1,0:T(8,128)} %get-tuple-element.4) | data formatting | bytes 1048576 | tf_op jit(solution)/shard_map/reshape | solution.py:518
  73.5 1.8 %reshape.19 = f32[1,2,16,2,1024]{4,3,2,1,0:T(2,128)} reshape(f32[2,32,1024]{2,1,0:T(8,128)} %get-tuple-element.5) | data formatting | bytes 524288 | tf_op jit(solution)/shard_map/reshape | solution.py:518
where the time goes:
time: 75.5 us; the launch traced here: 75.3 us
  Pallas kernels  66.7 us (88%)
  local copies, waits for them, and re-layouts  7.96 us (11%)
    pallas_call x1, Pallas kernels, per_device(): pl.pallas_call(kernel, out_shape=(jax.ShapeDtypeStruct((2, 64, 1024), F32...  66.7 us
    reshape x2, local copies, waits for them, and re-layouts, per_device(): return (out_g.reshape(2, 32, 2, 1024), out_v.reshape(1, 2, 16, 2, 1024))  3.94 us
    reshape x1, local copies, waits for them, and re-layouts, per_device(): green.reshape(2, 64, 1024)  2.19 us
    reshape x1, local copies, waits for them, and re-layouts, per_device(): inter.reshape(2, 32, 1024)  1.83 us

commit v1 on v0

--- a/solution.py
+++ b/solution.py
@@ -196,10 +196,9 @@
 PAIRS = ((1, 7, 2), (2, 6, 4), (3, 5, 6))
 
 
-def sheet_there(x, table, out):
-    rows = x.shape[1]
-    re = [x[0, :, 128 * g : 128 * g + 128] for g in range(8)]
-    im = [x[1, :, 128 * g : 128 * g + 128] for g in range(8)]
+def sheet_there(x, plane, rows, table, out):
+    re = [x[0, pl.ds(2 * g + plane, rows, 16), :] for g in range(8)]
+    im = [x[1, pl.ds(2 * g + plane, rows, 16), :] for g in range(8)]
     yr, yi = eight(re, im, 1)
     first = lax.broadcasted_iota(jnp.int32, (rows, 256), 1) % 8 < 4
 
@@ -219,8 +218,7 @@
         put(group + 1, jnp.where(first, b, a))
 
 
-def sheet_back(x, table, out):
-    rows = x.shape[2]
+def sheet_back(x, plane, rows, table, out):
     first = lax.broadcasted_iota(jnp.int32, (rows, 256), 1) % 8 < 4
     held = [None] * 8
 
@@ -239,8 +237,8 @@
         im.append(y[:, 128:])
     re, im = eight(re, im, -1)
     for g in range(8):
-        out[0, :, 128 * g : 128 * g + 128] = re[g]
-        out[1, :, 128 * g : 128 * g + 128] = im[g]
+        out[0, pl.ds(2 * g + plane, rows, 16), :] = re[g]
+        out[1, pl.ds(2 * g + plane, rows, 16), :] = im[g]
 
 
 def swap_parts(x, sign):
@@ -271,25 +269,14 @@
     self_y = jnp.where(o % 8 == 0, 1, 0)
 
     loads = {}
-    for k, (name, src, dst) in enumerate(
-        [
-            ("x_g", green, x_g),
-            ("sheet", sheet_h, sheet),
-            ("x_v", inter, x_v),
-            ("whole", whole_h.at[parity], whole),
-            ("fermi", fermi_h, fermi),
-            ("mirror", mirror_h.at[parity * 4 + self_x * 2 + self_y], mirror),
-            ("boseb", boseb_h, boseb),
-            ("partsb", partsb_h.at[parity], partsb),
-            ("parts", parts_h.at[parity], parts),
-            ("bose", bose_h, bose),
-            ("fermib", fermib_h, fermib),
-            ("wholeb", wholeb_h.at[parity], wholeb),
-            ("sheetb", sheetb_h, sheetb),
-        ]
-    ):
-        loads[name] = pltpu.make_async_copy(src, dst, load_sem.at[k])
+
+    def load(name, src, dst):
+        loads[name] = pltpu.make_async_copy(src, dst, load_sem.at[len(loads)])
         loads[name].start()
+
+    load("x_g", green, x_g)
+    load("sheet", sheet_h, sheet)
+    load("x_v", inter, x_v)
 
     def z_peer(d):
         other = (z + d) % 8
@@ -337,7 +324,7 @@
 
         return wait
 
-    def exchange_o(src_at, dst_at, src_31, dst_31):
+    def exchange_o(src_at, dst_at, some):
         s, r, l = new_sem(), new_sem(), new_sem()
         own = pltpu.make_async_copy(src_at(o), dst_at(o), l)
 
@@ -351,7 +338,7 @@
         lax.fori_loop(1, 32, send, 0)
         own.start()
         rest = pltpu.make_async_remote_copy(
-            src_31, dst_31, s, r, device_id=o_peer(1)[1], device_id_type=MESH
+            some, some, s, r, device_id=o_peer(1)[1], device_id_type=MESH
         )
         sent.append(rest)
 
@@ -361,54 +348,66 @@
 
         return wait
 
-    def rows_at(ref):
-        def at(k):
-            piece = pl.ds(pl.multiple_of(k * 8, 8), 8)
-            return ref.at[:, :, piece, :] if len(ref.shape) == 4 else ref.at[:, piece, :]
-
-        return at
-
-    def planes_at(ref):
-        def at(k):
-            planes = pl.ds(2 * (k // 4), 2)
-            lanes = pl.ds(pl.multiple_of((k % 4) * 128, 128), 128)
-            return ref.at[:, planes, :, lanes] if len(ref.shape) == 4 else ref.at[planes, :, lanes]
-
-        return at
-
-    def rows_31(ref):
-        return ref.at[:, :, pl.ds(0, 248), :] if len(ref.shape) == 4 else ref.at[:, pl.ds(0, 248), :]
+    def rows_g(ref, b):
+        return lambda k: ref.at[b, :, pl.ds(pl.multiple_of(k * 8, 8), 8), :]
+
+    def rows_v(ref, b):
+        return lambda k: ref.at[b, pl.ds(pl.multiple_of(k * 8, 8), 8), :]
+
+    def planes_g(ref, b):
+        return lambda k: ref.at[:, 2 * (k // 4) + b, :, pl.ds(pl.multiple_of((k % 4) * 128, 128), 128)]
+
+    def planes_v(ref, b):
+        return lambda k: ref.at[2 * (k // 4) + b, :, pl.ds(pl.multiple_of((k % 4) * 128, 128), 128)]
+
+    def some_g(ref, b):
+        return ref.at[b, :, pl.ds(0, 248), :]
+
+    def some_v(ref, b):
+        return ref.at[b, pl.ds(0, 248), :]
 
     loads["x_g"].wait()
     loads["sheet"].wait()
-    sheet_there(x_g, sheet, sa_g)
-    pl.semaphore_wait(barrier, 38)
-    a_g = exchange_z(sa_g, ra_g)
+    a_g, a_v, b_g, b_v, c_g, c_v, d_g, d_v = [[None, None] for _ in range(8)]
+    for b in range(2):
+        sheet_there(x_g, b, 32, sheet, sa_g.at[b])
+        if b == 0:
+            pl.semaphore_wait(barrier, 38)
+        a_g[b] = exchange_z(sa_g.at[b], ra_g.at[b])
     loads["x_v"].wait()
-    sheet_there(x_v, sheet, sa_v)
-    a_v = exchange_z(sa_v, ra_v)
-
-    a_g()
-    for p in range(2):
-        for b in range(2):
-            even = jnp.concatenate([ra_g[2 * h, p, pl.ds(b, 32, 2), :] for h in range(4)], 0)
-            odd = jnp.concatenate([ra_g[2 * h + 1, p, pl.ds(b, 32, 2), :] for h in range(4)], 0)
-            sb_g[p, b, :128, :] = (even + odd).T
-            sb_g[p, b, 128:, :] = (even - odd).T
-    b_g = exchange_o(rows_at(sb_g), planes_at(rb_g), rows_31(sb_g), rows_31(ub_g))
-    a_v()
-    for b in range(2):
-        even = jnp.concatenate(
-            [ra_v[2 * h, p, pl.ds(b, 16, 2), :] for p in range(2) for h in range(4)], 0
-        )
-        odd = jnp.concatenate(
-            [ra_v[2 * h + 1, p, pl.ds(b, 16, 2), :] for p in range(2) for h in range(4)], 0
-        )
+    for b in range(2):
+        sheet_there(x_v, b, 16, sheet, sa_v.at[b])
+        a_v[b] = exchange_z(sa_v.at[b], ra_v.at[b])
+
+    load("whole", whole_h.at[parity], whole)
+    load("fermi", fermi_h, fermi)
+    load("mirror", mirror_h.at[parity * 4 + self_x * 2 + self_y], mirror)
+    load("boseb", boseb_h, boseb)
+    load("partsb", partsb_h.at[parity], partsb)
+    load("parts", parts_h.at[parity], parts)
+    load("bose", bose_h, bose)
+    load("fermib", fermib_h, fermib)
+    load("wholeb", wholeb_h.at[parity], wholeb)
+    load("sheetb", sheetb_h, sheetb)
+
+    for b in range(2):
+        a_g[b]()
+        for p in range(2):
+            even = jnp.concatenate([ra_g[b, 2 * h, p] for h in range(4)], 0)
+            odd = jnp.concatenate([ra_g[b, 2 * h + 1, p] for h in range(4)], 0)
+            sb_g[b, p, :128, :] = (even + odd).T
+            sb_g[b, p, 128:, :] = (even - odd).T
+        b_g[b] = exchange_o(rows_g(sb_g, b), planes_g(rb_g, b), some_g(ub_g, b))
+    for b in range(2):
+        a_v[b]()
+        even = jnp.concatenate([ra_v[b, 2 * h, p] for p in range(2) for h in range(4)], 0)
+        odd = jnp.concatenate([ra_v[b, 2 * h + 1, p] for p in range(2) for h in range(4)], 0)
         sb_v[b, :128, :] = (even + odd).T
         sb_v[b, 128:, :] = (even - odd).T
-    b_v = exchange_o(rows_at(sb_v), planes_at(rb_v), rows_31(sb_v), rows_31(ub_v))
-
-    b_g()
+        b_v[b] = exchange_o(rows_v(sb_v, b), planes_v(rb_v, b), some_v(ub_v, b))
+
+    b_g[0]()
+    b_g[1]()
     loads["whole"].wait()
     lattice = table_by_data((whole[0], whole[1]), rb_g[...].reshape(256, 512))
     loads["fermi"].wait()
@@ -430,9 +429,11 @@
     loads["partsb"].wait()
     cs = table_by_data((partsb[0], partsb[1]), nu)
     tb_v[...] = (cs[:128] + swap_parts(cs[128:], -1)).reshape(16, 8, 512)
-    c_v = exchange_o(planes_at(tb_v), rows_at(ub_v), rows_31(sb_v), rows_31(ub_v))
-
-    b_v()
+    for b in range(2):
+        c_v[b] = exchange_o(planes_v(tb_v, b), rows_v(ub_v, b), some_v(ub_v, b))
+
+    b_v[0]()
+    b_v[1]()
     loads["parts"].wait()
     cs = table_by_data((parts[0], parts[1]), rb_v[...].reshape(128, 512))
     loads["bose"].wait()
@@ -454,33 +455,36 @@
     )
     loads["wholeb"].wait()
     tb_g[...] = table_by_data((wholeb[0], wholeb[1]), omega).reshape(2, 16, 8, 512)
-    c_g = exchange_o(planes_at(tb_g), rows_at(ub_g), rows_31(sb_g), rows_31(ub_g))
-
-    c_v()
-    for b in range(2):
+    for b in range(2):
+        c_g[b] = exchange_o(planes_g(tb_g, b), rows_g(ub_g, b), some_g(ub_g, b))
+
+    for b in range(2):
+        c_v[b]()
         even, odd = ub_v[b, :128, :].T, ub_v[b, 128:, :].T
         for lo, value in ((0, even + odd), (1, even - odd)):
             for p in range(2):
                 for h in range(4):
                     k = 64 * p + 16 * h
-                    ta_v[2 * h + lo, p, pl.ds(b, 16, 2), :] = value[k : k + 16]
-    d_v = exchange_z(ta_v, ua_v)
-    c_g()
-    for p in range(2):
-        for b in range(2):
-            even, odd = ub_g[p, b, :128, :].T, ub_g[p, b, 128:, :].T
+                    ta_v[b, 2 * h + lo, p] = value[k : k + 16]
+        d_v[b] = exchange_z(ta_v.at[b], ua_v.at[b])
+    for b in range(2):
+        c_g[b]()
+        for p in range(2):
+            even, odd = ub_g[b, p, :128, :].T, ub_g[b, p, 128:, :].T
             for lo, value in ((0, even + odd), (1, even - odd)):
                 for h in range(4):
-                    ta_g[2 * h + lo, p, pl.ds(b, 32, 2), :] = value[32 * h : 32 * h + 32]
-    d_g = exchange_z(ta_g, ua_g)
-
-    d_v()
+                    ta_g[b, 2 * h + lo, p] = value[32 * h : 32 * h + 32]
+        d_g[b] = exchange_z(ta_g.at[b], ua_g.at[b])
+
     loads["sheetb"].wait()
-    sheet_back(ua_v, sheetb, y_v)
+    for b in range(2):
+        d_v[b]()
+        sheet_back(ua_v.at[b], b, 16, sheetb, y_v)
     put_v = pltpu.make_async_copy(y_v, out_v, load_sem.at[13])
     put_v.start()
-    d_g()
-    sheet_back(ua_g, sheetb, y_g)
+    for b in range(2):
+        d_g[b]()
+        sheet_back(ua_g.at[b], b, 32, sheetb, y_g)
     put_g = pltpu.make_async_copy(y_g, out_g, load_sem.at[14])
     put_g.start()
     for copy in sent:
@@ -489,15 +493,25 @@
     put_g.wait()
 
 
+def view(x):
+    n = x.shape[-3]
+    return x.reshape(2, n, 2, 8, 128).transpose(0, 1, 3, 2, 4).reshape(2, n * 16, 128)
+
+
+def unview(x):
+    n = x.shape[1] // 16
+    return x.reshape(2, n, 8, 2, 128).transpose(0, 1, 3, 2, 4).reshape(2, n, 2, 1024)
+
+
 def per_device(green, inter):
     shapes = [
-        (2, 64, 1024), (2, 32, 1024),
+        (2, 512, 128), (2, 256, 128),
         (2, 8, 256, 256), (2, 8, 256, 256), (2, 256, 256), (2, 256, 256), (2, 256, 128), (2, 256, 128),
         (2, 512, 512), (2, 512, 512), (2, 512, 1024), (2, 1024, 512), (128, 128),
-        (8, 2, 64, 128), (8, 2, 32, 128), (8, 2, 64, 128), (8, 2, 32, 128),
+        (2, 8, 2, 32, 128), (2, 8, 2, 16, 128), (2, 8, 2, 32, 128), (2, 8, 2, 16, 128),
         (2, 2, 256, 128), (2, 256, 128), (2, 16, 8, 512), (16, 8, 512), (128, 1024),
         (2, 16, 8, 512), (16, 8, 512), (2, 2, 256, 128), (2, 256, 128),
-        (8, 2, 64, 128), (8, 2, 32, 128), (8, 2, 64, 128), (8, 2, 32, 128), (2, 64, 1024), (2, 32, 1024),
+        (2, 8, 2, 32, 128), (2, 8, 2, 16, 128), (2, 8, 2, 32, 128), (2, 8, 2, 16, 128), (2, 512, 128), (2, 256, 128),
     ]
     scratch = [pltpu.VMEM(s, BF16 if 2 <= k < 13 else F32) for k, s in enumerate(shapes)]
     any_spec = pl.BlockSpec(memory_space=pl.ANY)
@@ -505,17 +519,17 @@
     out_g, out_v = pl.pallas_call(
         kernel,
         out_shape=(
-            jax.ShapeDtypeStruct((2, 64, 1024), F32),
-            jax.ShapeDtypeStruct((2, 32, 1024), F32),
+            jax.ShapeDtypeStruct((2, 512, 128), F32),
+            jax.ShapeDtypeStruct((2, 256, 128), F32),
         ),
         in_specs=[any_spec] * (2 + len(constants)),
         out_specs=(any_spec, any_spec),
-        scratch_shapes=scratch + [pltpu.SemaphoreType.DMA((15,)), pltpu.SemaphoreType.DMA((24,))],
+        scratch_shapes=scratch + [pltpu.SemaphoreType.DMA((15,)), pltpu.SemaphoreType.DMA((48,))],
         compiler_params=pltpu.CompilerParams(
             collective_id=0, has_side_effects=True, vmem_limit_bytes=56 << 20
         ),
-    )(green.reshape(2, 64, 1024), inter.reshape(2, 32, 1024), *constants)
-    return out_g.reshape(2, 32, 2, 1024), out_v.reshape(1, 2, 16, 2, 1024)
+    )(view(green), view(inter), *constants)
+    return unview(out_g), unview(out_v)[None]
 
 
 def solution(mesh):

time: 75.5 us -> 67 us (0.89)
  local copies, waits for them, and re-layouts: 7.96 us -> 3.54 us
  Pallas kernels: 66.7 us -> 62.7 us
    reshape x4 -> x0, local copies, waits for them, and re-layouts: 7.96 us -> none  [the longest x2 3.94 us: per_device(): return (out_g.reshape(2, 32, 2, 1024), out_v.reshape(1, 2, 16, 2, 1024))]
    pallas_call x1, Pallas kernels: 66.7 us -> 62.7 us  [per_device(): pl.pallas_call(kernel, out_shape=(jax.ShapeDtypeStruct((2, 512, 128), F32...]
    unnamed x0 -> x2, local copies, waits for them, and re-layouts: none -> 3.54 us
where the time goes in v1:
time: 67 us; the launch traced here: 66.8 us
  Pallas kernels  62.7 us (94%)
  local copies, waits for them, and re-layouts  3.54 us (5%)
    pallas_call x1, Pallas kernels, per_device(): pl.pallas_call(kernel, out_shape=(jax.ShapeDtypeStruct((2, 512, 128), F32...  62.7 us
    unnamed x2, local copies, waits for them, and re-layouts  3.54 us

profile of v1, /device:TPU:1, one launch (start us, length us, event | category | flops | bytes accessed | tf_op | source)
XLA Modules:
  0.0 66.8 jit_solution(14422727414483931222)
XLA Ops:
  0.6 62.7 %shard_map.140 = (f32[2,512,128]{2,1,0:T(8,128)}, f32[2,256,128]{2,1,0:T(8,128)}) custom-call(f32[2,512,128]{2,1,0:T(8,128)} %bitcast.20, f32[2,256,128]{2,1,0:T(8,128)} %bitcast.22, bf16[2,8,256,256]{3,2,1,0:T(8,128)(2,1)} %constant.22.clone.sheet_h, bf16[2,8,256,256]{3,2,1,0:T(8,128)(2,1)} %constant.23.clone.sheetb_h, ...), custom_call_target="tpu_custom_call" | custom-call | tf_op jit(solution)/shard_map/pallas_call | solution.py:519
  63.3 1.9 %copy.21 = f32[2,32,2,1024]{3,2,1,0:T(2,128)} copy(f32[2,32,2,1024]{3,2,1,0:T(2,128)} %bitcast.21) | data formatting | bytes 1048576
  65.2 1.7 %copy.22 = f32[1,2,16,2,1024]{4,3,2,1,0:T(2,128)} copy(f32[1,2,16,2,1024]{4,3,2,1,0:T(2,128)} %bitcast.23) | data formatting | bytes 524288

commit v2 on v1

--- a/solution.py
+++ b/solution.py
@@ -133,8 +133,8 @@
         [parts[:, :128].transpose(0, 2, 1), parts[:, 128:].transpose(0, 2, 1)], 1
     )
     return (
-        split_table(sheet),
-        split_table(sheet.transpose(0, 2, 1)),
+        np.ascontiguousarray(split_table(sheet).swapaxes(0, 1)),
+        np.ascontiguousarray(split_table(sheet.transpose(0, 2, 1)).swapaxes(0, 1)),
         np.ascontiguousarray(split_table(whole).swapaxes(0, 1)),
         np.ascontiguousarray(split_table(whole.transpose(0, 2, 1)).swapaxes(0, 1)),
         np.ascontiguousarray(split_table(parts).swapaxes(0, 1)),
@@ -193,18 +193,25 @@
     )
 
 
+FAR_FIRST = sorted(
+    [(dx, dy, dc) for dx in range(4) for dy in range(4) for dc in range(2) if dx + dy + dc],
+    key=lambda t: -(10 * min(t[0], 4 - t[0]) + 10 * min(t[1], 4 - t[1]) + t[2]),
+)
+ORDER = (0, 4, 1, 7, 2, 6, 3, 5)
 PAIRS = ((1, 7, 2), (2, 6, 4), (3, 5, 6))
 
 
-def sheet_there(x, plane, rows, table, out):
+def sheet_there(x, plane, rows, table, out, loads=None):
     re = [x[0, pl.ds(2 * g + plane, rows, 16), :] for g in range(8)]
     im = [x[1, pl.ds(2 * g + plane, rows, 16), :] for g in range(8)]
     yr, yi = eight(re, im, 1)
     first = lax.broadcasted_iota(jnp.int32, (rows, 256), 1) % 8 < 4
 
     def one(residue):
+        if loads is not None:
+            loads["sheet" + str(residue)].wait()
         both = jnp.concatenate([yr[residue], yi[residue]], 1)
-        return data_by_table(both, (table[0, residue], table[1, residue]))
+        return data_by_table(both, (table[residue, 0], table[residue, 1]))
 
     def put(group, value):
         out[group, 0] = value[:, :128]
@@ -232,7 +239,7 @@
         held[n] = jnp.where(first, b, a)
     re, im = [], []
     for residue in range(8):
-        y = data_by_table(held[residue], (table[0, residue], table[1, residue]))
+        y = data_by_table(held[residue], (table[residue, 0], table[residue, 1]))
         re.append(y[:, :128])
         im.append(y[:, 128:])
     re, im = eight(re, im, -1)
@@ -274,8 +281,10 @@
         loads[name] = pltpu.make_async_copy(src, dst, load_sem.at[len(loads)])
         loads[name].start()
 
-    load("x_g", green, x_g)
-    load("sheet", sheet_h, sheet)
+    for p in range(2):
+        load("x_g" + str(p), green.at[p], x_g.at[p])
+    for residue in ORDER:
+        load("sheet" + str(residue), sheet_h.at[residue], sheet.at[residue])
     load("x_v", inter, x_v)
 
     def z_peer(d):
@@ -286,6 +295,11 @@
         other = (o + d) % 32
         return other, {"kz": z_lo * 8 + other // 4, "freq": z_hi * 4 + other % 4}
 
+    def near(dx, dy, dc):
+        c2 = ((c // 2 + dx) % 4) * 2 + (c + dc) % 2
+        y2 = (y + dy) % 4
+        return c2 * 4 + y2, {"kz": z_lo * 8 + c2, "freq": z_hi * 4 + y2}
+
     barrier = pltpu.get_barrier_semaphore()
     for d in range(1, 8):
         pl.semaphore_signal(barrier, inc=1, device_id=z_peer(d)[1], device_id_type=MESH)
@@ -307,7 +321,7 @@
     def exchange_z(src, dst):
         s, r, l = new_sem(), new_sem(), new_sem()
         own = pltpu.make_async_copy(src.at[z], dst.at[z], l)
-        for d in (1, 7, 2, 6, 3, 5, 4):
+        for d in (4, 3, 5, 2, 6, 1, 7):
             other, device = z_peer(d)
             pltpu.make_async_remote_copy(
                 src.at[other], dst.at[z], s, r, device_id=device, device_id_type=MESH
@@ -328,14 +342,11 @@
         s, r, l = new_sem(), new_sem(), new_sem()
         own = pltpu.make_async_copy(src_at(o), dst_at(o), l)
 
-        def send(d, carry):
-            other, device = o_peer(d)
+        for dx, dy, dc in FAR_FIRST:
+            other, device = near(dx, dy, dc)
             pltpu.make_async_remote_copy(
                 src_at(other), dst_at(o), s, r, device_id=device, device_id_type=MESH
             ).start()
-            return carry
-
-        lax.fori_loop(1, 32, send, 0)
         own.start()
         rest = pltpu.make_async_remote_copy(
             some, some, s, r, device_id=o_peer(1)[1], device_id_type=MESH
@@ -366,11 +377,11 @@
     def some_v(ref, b):
         return ref.at[b, pl.ds(0, 248), :]
 
-    loads["x_g"].wait()
-    loads["sheet"].wait()
+    loads["x_g0"].wait()
+    loads["x_g1"].wait()
     a_g, a_v, b_g, b_v, c_g, c_v, d_g, d_v = [[None, None] for _ in range(8)]
     for b in range(2):
-        sheet_there(x_g, b, 32, sheet, sa_g.at[b])
+        sheet_there(x_g, b, 32, sheet, sa_g.at[b], loads if b == 0 else None)
         if b == 0:
             pl.semaphore_wait(barrier, 38)
         a_g[b] = exchange_z(sa_g.at[b], ra_g.at[b])
@@ -480,17 +491,36 @@
     for b in range(2):
         d_v[b]()
         sheet_back(ua_v.at[b], b, 16, sheetb, y_v)
-    put_v = pltpu.make_async_copy(y_v, out_v, load_sem.at[13])
+    put_v = pltpu.make_async_copy(y_v, out_v, load_sem.at[30])
     put_v.start()
     for b in range(2):
         d_g[b]()
         sheet_back(ua_g.at[b], b, 32, sheetb, y_g)
-    put_g = pltpu.make_async_copy(y_g, out_g, load_sem.at[14])
-    put_g.start()
+    puts = [pltpu.make_async_copy(y_g.at[p, pl.ds(256 * h, 256)], out_g.at[p, pl.ds(256 * h, 256)], load_sem.at[31 + 2 * p + h]) for p in range(2) for h in range(2)]
+    for put in puts:
+        put.start()
     for copy in sent:
         copy.wait_send()
     put_v.wait()
-    put_g.wait()
+    for put in puts:
+        put.wait()
+
+
+def hand_on(g, v, out_g, out_v, held_g, held_v, sem):
+    ways = []
+    for p in range(2):
+        for half in range(2):
+            ways.append([r.at[p, pl.ds(256 * half, 256)] for r in (g, held_g, out_g)])
+        ways.append([r.at[p] for r in (v, held_v, out_v)])
+    first = [pltpu.make_async_copy(a, b, sem.at[k]) for k, (a, b, _) in enumerate(ways)]
+    second = [pltpu.make_async_copy(b, c, sem.at[6 + k]) for k, (_, b, c) in enumerate(ways)]
+    for copy in first:
+        copy.start()
+    for there, back in zip(first, second):
+        there.wait()
+        back.start()
+    for copy in second:
+        copy.wait()
 
 
 def view(x):
@@ -506,7 +536,7 @@
 def per_device(green, inter):
     shapes = [
         (2, 512, 128), (2, 256, 128),
-        (2, 8, 256, 256), (2, 8, 256, 256), (2, 256, 256), (2, 256, 256), (2, 256, 128), (2, 256, 128),
+        (8, 2, 256, 256), (8, 2, 256, 256), (2, 256, 256), (2, 256, 256), (2, 256, 128), (2, 256, 128),
         (2, 512, 512), (2, 512, 512), (2, 512, 1024), (2, 1024, 512), (128, 128),
         (2, 8, 2, 32, 128), (2, 8, 2, 16, 128), (2, 8, 2, 32, 128), (2, 8, 2, 16, 128),
         (2, 2, 256, 128), (2, 256, 128), (2, 16, 8, 512), (16, 8, 512), (128, 1024),
@@ -524,11 +554,22 @@
         ),
         in_specs=[any_spec] * (2 + len(constants)),
         out_specs=(any_spec, any_spec),
-        scratch_shapes=scratch + [pltpu.SemaphoreType.DMA((15,)), pltpu.SemaphoreType.DMA((48,))],
+        scratch_shapes=scratch + [pltpu.SemaphoreType.DMA((36,)), pltpu.SemaphoreType.DMA((48,))],
         compiler_params=pltpu.CompilerParams(
             collective_id=0, has_side_effects=True, vmem_limit_bytes=56 << 20
         ),
     )(view(green), view(inter), *constants)
+    out_g, out_v = pl.pallas_call(
+        hand_on,
+        out_shape=(jax.ShapeDtypeStruct((2, 512, 128), F32), jax.ShapeDtypeStruct((2, 256, 128), F32)),
+        in_specs=[any_spec] * 2,
+        out_specs=(any_spec, any_spec),
+        scratch_shapes=[
+            pltpu.VMEM((2, 512, 128), F32),
+            pltpu.VMEM((2, 256, 128), F32),
+            pltpu.SemaphoreType.DMA((12,)),
+        ],
+    )(out_g, out_v)
     return unview(out_g), unview(out_v)[None]
 
 

time: 67 us -> 63.3 us (0.945)
  local copies, waits for them, and re-layouts: 3.54 us -> 0 us
    unnamed x2 -> x0, local copies, waits for them, and re-layouts: 3.54 us -> none
    pallas_call x1, Pallas kernels: 62.7 us -> 60.6 us  [per_device(): pl.pallas_call(kernel, out_shape=(jax.ShapeDtypeStruct((2, 512, 128), F32...]
    pallas_call x0 -> x1, Pallas kernels: none -> 1.97 us  [per_device(): pl.pallas_call(hand_on, out_shape=(jax.ShapeDtypeStruct((2, 512, 128), F3...]
where the time goes in v2:
time: 63.3 us; the launch traced here: 63.2 us
  Pallas kernels  62.6 us (99%)
  between operations  0.64 us (1%)
    pallas_call x1, Pallas kernels, per_device(): pl.pallas_call(kernel, out_shape=(jax.ShapeDtypeStruct((2, 512, 128), F32...  60.6 us
    pallas_call x1, Pallas kernels, per_device(): pl.pallas_call(hand_on, out_shape=(jax.ShapeDtypeStruct((2, 512, 128), F3...  1.97 us

profile of v2, /device:TPU:1, one launch (start us, length us, event | category | flops | bytes accessed | tf_op | source)
XLA Modules:
  0.0 63.2 jit_solution(13548811490898574290)
XLA Ops:
  0.6 60.6 %shard_map.140 = (f32[2,512,128]{2,1,0:T(8,128)}, f32[2,256,128]{2,1,0:T(8,128)}) custom-call(f32[2,512,128]{2,1,0:T(8,128)} %bitcast.20, f32[2,256,128]{2,1,0:T(8,128)} %bitcast.21, bf16[8,2,256,256]{3,2,1,0:T(8,128)(2,1)} %constant.22.clone.sheet_h, bf16[8,2,256,256]{3,2,1,0:T(8,128)(2,1)} %constant.23.clone.sheetb_h, ...), custom_call_target="tpu_custom_call" | custom-call | tf_op jit(solution)/shard_map/pallas_call | solution.py:549
  61.2 2.0 %shard_map.141 = (f32[2,512,128]{2,1,0:T(8,128)}, f32[2,256,128]{2,1,0:T(8,128)}) custom-call(f32[2,512,128]{2,1,0:T(8,128)} %get-tuple-element.6.g, f32[2,256,128]{2,1,0:T(8,128)} %get-tuple-element.7.v), custom_call_target="tpu_custom_call" | custom-call | tf_op jit(solution)/shard_map/pallas_call | solution.py:562

commit v3 on v2

v3 whole, which is shorter than its diff:
```python
import functools
import math

import jax
import jax.numpy as jnp
import ml_dtypes
import numpy as np
from jax import lax
from jax.experimental import pallas as pl
from jax.experimental.pallas import tpu as pltpu
from jax.sharding import PartitionSpec as P

MESH = pl.DeviceIdType.MESH
F32 = jnp.float32
BF16 = jnp.bfloat16


def split_table(table):
    high = table.astype(ml_dtypes.bfloat16)
    low = (table - high.astype(np.float64)).astype(ml_dtypes.bfloat16)
    return np.stack([high, low])


def pairs_of(group):
    ys = range(32)

    def with_x(x):
        return [((x, y), ((32 - x) % 32, (32 - y) % 32)) for y in ys]

    if group == 0:
        pairs = []
        for x in (0, 16):
            pairs += [((x, 0), (x, 16))] + [((x, y), (x, 32 - y)) for y in range(1, 16)]
        return pairs + with_x(8)
    if group == 1:
        return with_x(4) + with_x(12)
    m = group // 2
    if group % 2 == 0:
        return with_x(m) + with_x(m + 8)
    return with_x(16 - m) + with_x(8 - m)


def columns(residue):
    if residue in (0, 4):
        return np.array(pairs_of(residue // 4))
    m = min(residue, 8 - residue)
    a, b = np.array(pairs_of(2 * m)), np.array(pairs_of(2 * m + 1))
    if residue < 4:
        return np.stack([a[:, 0], b[:, 1]], 1)
    return np.stack([b[:, 0], a[:, 1]], 1)


def sheet_tables():
    tables = []
    xl = np.repeat(np.arange(4), 32)
    ky = np.tile(np.arange(32), 4)
    for residue in range(8):
        site = columns(residue).reshape(2, 2, 16, 2, 2).transpose(0, 2, 1, 3, 4)
        x, y = site[..., 0], site[..., 1]
        assert (x % 8 == residue).all()
        turns = xl[:, None, None, None, None] * x + ky[:, None, None, None, None] * y
        angle = 2 * np.pi * (turns % 32) / 32
        c, s = np.cos(angle) / 32, np.sin(angle) / 32
        real = np.stack([c, s], 4)
        imag = np.stack([-s, c], 4)
        tables.append(np.concatenate([real, imag], 0).reshape(256, 256))
    return np.stack(tables)


def depth_tables():
    whole = np.zeros((2, 2, 16, 2, 16, 2, 2))
    kappa = np.arange(16)
    for parity in range(2):
        depth = 2 * np.arange(16) + parity
        angle = 2 * np.pi * ((depth[:, None] * kappa) % 32) / 32
        c, s = np.cos(angle) / math.sqrt(32), np.sin(angle) / math.sqrt(32)
        for e in range(2):
            whole[parity, 0, :, e, :, 0, e] = c
            whole[parity, 0, :, e, :, 1, e] = -s
            whole[parity, 1, :, e, :, 0, e] = s
            whole[parity, 1, :, e, :, 1, e] = c
    return whole.reshape(2, 64, 64)


def angles(length, offset):
    p = 2 * np.arange(length) - length + offset
    j = np.arange(256)
    return 2 * np.pi * ((p[:, None] * (2 * j + 1)) % 2048) / 2048


def fermi_table():
    theta = angles(512, 1).reshape(4, 4, 32, 256).transpose(1, 0, 2, 3).reshape(512, 256)
    return np.concatenate([np.cos(theta), np.sin(theta)], 1) / math.sqrt(512)


def bose_table():
    theta = angles(256, 0).reshape(4, 4, 16, 256).transpose(1, 0, 2, 3)
    table = np.zeros((2, 4, 2, 4, 16, 512))
    for parity in range(2):
        table[parity, :, parity] = np.concatenate([np.cos(theta), np.sin(theta)], -1)
    return table.reshape(2, 512, 512)


def mirror_tables():
    tables = np.zeros((2, 2, 32, 128))
    for parity in range(2):
        for same in range(2):
            for depth in range(16):
                other = (-depth - parity) % 16
                for e in range(2):
                    tables[parity, same, 2 * depth + e, 2 * other + (e if same else 1 - e)] = 1
    return tables.astype(ml_dtypes.bfloat16)


def by_parity(table):
    columns = max(128, table.shape[-1])
    wide = np.zeros(table.shape[:-1] + (columns,))
    wide[..., : table.shape[-1]] = table
    return np.ascontiguousarray(split_table(wide).swapaxes(0, 1))


@functools.cache
def tables():
    sheet = sheet_tables()
    whole = depth_tables()
    fermi = fermi_table()
    bose = bose_table()
    return (
        by_parity(sheet),
        by_parity(sheet.transpose(0, 2, 1)),
        by_parity(whole),
        by_parity(whole.transpose(0, 2, 1)),
        split_table(fermi),
        split_table(fermi.T),
        by_parity(bose / 16),
        by_parity(bose.transpose(0, 2, 1) / math.sqrt(512)),
        mirror_tables(),
    )


def split(x):
    high = x.astype(BF16)
    return high, (x - high.astype(F32)).astype(BF16)


def dot(a, b):
    return jnp.dot(a, b, preferred_element_type=F32)


def data_by_table(x, high_table, low_table):
    n = x.shape[0]
    high, low = split(x)
    both = dot(jnp.concatenate([high, low], 0), high_table)
    return both[:n] + both[n:] + dot(high, low_table)


def table_by_data(table, x):
    n, k = table.shape[1], x.shape[0]
    high, low = split(x)
    stacked = table[...].reshape(2 * n, 128)[:, :k]
    both = dot(stacked, high)
    return both[:n] + both[n:] + dot(stacked[:n], low)


def four(re, im, sign):
    s0r, s0i = re[0] + re[2], im[0] + im[2]
    d0r, d0i = re[0] - re[2], im[0] - im[2]
    s1r, s1i = re[1] + re[3], im[1] + im[3]
    d1r, d1i = re[1] - re[3], im[1] - im[3]
    tr, ti = (-d1i, d1r) if sign > 0 else (d1i, -d1r)
    return [s0r + s1r, d0r + tr, s0r - s1r, d0r - tr], [s0i + s1i, d0i + ti, s0i - s1i, d0i - ti]


def eight(re, im, sign):
    er, ei = four(re[0::2], im[0::2], sign)
    orr, oi = four(re[1::2], im[1::2], sign)
    h = math.sqrt(0.5)
    tr = [orr[0]]
    ti = [oi[0]]
    if sign > 0:
        tr += [h * (orr[1] - oi[1]), -oi[2], -h * (orr[3] + oi[3])]
        ti += [h * (orr[1] + oi[1]), orr[2], h * (orr[3] - oi[3])]
    else:
        tr += [h * (orr[1] + oi[1]), oi[2], h * (oi[3] - orr[3])]
        ti += [h * (oi[1] - orr[1]), -orr[2], -h * (orr[3] + oi[3])]
    return (
        [er[k] + tr[k] for k in range(4)] + [er[k] - tr[k] for k in range(4)],
        [ei[k] + ti[k] for k in range(4)] + [ei[k] - ti[k] for k in range(4)],
    )


FAR_FIRST = sorted(
    [(dx, dy, dc) for dx in range(4) for dy in range(4) for dc in range(2) if dx + dy + dc],
    key=lambda t: -(10 * min(t[0], 4 - t[0]) + 10 * min(t[1], 4 - t[1]) + t[2]),
)
ORDER = (0, 4, 1, 7, 2, 6, 3, 5)
PAIRS = ((1, 7, 2), (2, 6, 4), (3, 5, 6))


def lane(rows, columns):
    return lax.broadcasted_iota(jnp.int32, (rows, columns), 1)


def sheet_there(x_g, x_v, table, loads, out):
    def rows(p, g):
        return jnp.concatenate(
            [x[p, pl.ds(2 * g + b, n, 16), :] for b in range(2) for x, n in ((x_g, 32), (x_v, 16))], 0
        )

    yr, yi = eight([rows(0, g) for g in range(8)], [rows(1, g) for g in range(8)], 1)
    first = lane(96, 256) % 2 == 0
    plane = lane(48, 128) % 8 < 4

    def one(residue):
        loads["sheet" + str(residue)].wait()
        both = jnp.concatenate([yr[residue], yi[residue]], 1)
        return data_by_table(both, table[residue, 0], table[residue, 1])

    def put(group, value):
        for high in range(2):
            zero = value[:48, 128 * high : 128 * high + 128]
            one_ = value[48:, 128 * high : 128 * high + 128]
            out[2 * high, group] = jnp.where(plane, zero, pltpu.roll(one_, 4, 1))
            out[2 * high + 1, group] = jnp.where(plane, pltpu.roll(zero, 124, 1), one_)

    put(0, one(0))
    put(1, one(4))
    for m, n, group in PAIRS:
        a, b = one(m), one(n)
        put(group, jnp.where(first, a, b))
        put(group + 1, jnp.where(first, b, a))


def sheet_back(x, high, table):
    first = lane(96, 128) % 2 == 0
    plane = lane(48, 128) % 8 < 4

    def get(group):
        a, b = x[2 * high, group], x[2 * high + 1, group]
        return jnp.concatenate(
            [
                jnp.where(plane, a, pltpu.roll(b, 4, 1)),
                jnp.where(plane, pltpu.roll(a, 124, 1), b),
            ],
            0,
        )

    held = [None] * 8
    held[0], held[4] = get(0), get(1)
    for m, n, group in PAIRS:
        a, b = get(group), get(group + 1)
        held[m] = jnp.where(first, a, b)
        held[n] = jnp.where(first, b, a)
    part = pl.ds(128 * high, 128)
    return [data_by_table(held[k], table[k, 0, part, :], table[k, 1, part, :]) for k in range(8)]


def in_time(p, odd):
    ca, sa = p[:32, :256], p[:32, 256:]
    cb, sb = p[32:, :256], p[32:, 256:]
    if odd:
        return ca + sb, cb - sa, sb - ca, -(cb + sa)
    return ca + sb, cb - sa, ca - sb, cb + sa


def out_of_time(dr, di, er, ei):
    return jnp.concatenate([jnp.concatenate([dr, -ei], 1), jnp.concatenate([di, er], 1)], 0)


def kernel(
    green, inter, sheet_h, sheetb_h, whole_h, wholeb_h, fermi_h, fermib_h, bose_h, boseb_h, mirror_h,
    out_g, out_v,
    x_g, x_v, sheet, sheetb, whole, wholeb, fermi, fermib, bose, boseb, mirror,
    sa, ra, sb, rb, tb, ub, ta, ua, half, y_g, y_v, load_sem, put_sem, sem,
):
    kz, freq = lax.axis_index("kz"), lax.axis_index("freq")
    z_lo, c = kz // 8, kz % 8
    z_hi, y = freq // 4, freq % 4
    z = z_hi * 2 + z_lo
    o = c * 4 + y
    parity = o // 16

    loads = {}

    def load(name, src, dst):
        loads[name] = pltpu.make_async_copy(src, dst, load_sem.at[len(loads)])
        loads[name].start()

    for p in range(2):
        load("x_g" + str(p), green.at[p], x_g.at[p])
        load("x_v" + str(p), inter.at[p], x_v.at[p])
    for residue in ORDER:
        load("sheet" + str(residue), sheet_h.at[residue], sheet.at[residue])

    def z_peer(d):
        other = (z + d) % 8
        return other, {"kz": (other % 2) * 8 + c, "freq": (other // 2) * 4 + y}

    def near(dx, dy, dc):
        c2 = ((c // 2 + dx) % 4) * 2 + (c + dc) % 2
        y2 = (y + dy) % 4
        return c2 * 4 + y2, {"kz": z_lo * 8 + c2, "freq": z_hi * 4 + y2}

    barrier = pltpu.get_barrier_semaphore()
    for d in range(1, 8):
        pl.semaphore_signal(barrier, inc=1, device_id=z_peer(d)[1], device_id_type=MESH)
    for dx, dy, dc in FAR_FIRST:
        pl.semaphore_signal(barrier, inc=1, device_id=near(dx, dy, dc)[1], device_id_type=MESH)

    count = [0]

    def new_sem():
        count[0] += 1
        return sem.at[count[0] - 1]

    sent = []

    def exchange_z(src, dst):
        s, r, l = new_sem(), new_sem(), new_sem()
        own = pltpu.make_async_copy(src.at[z], dst.at[z], l)
        for d in (4, 3, 5, 2, 6, 1, 7):
            other, device = z_peer(d)
            pltpu.make_async_remote_copy(
                src.at[other], dst.at[z], s, r, device_id=device, device_id_type=MESH
            ).start()
        own.start()
        seven = pltpu.make_async_remote_copy(
            src.at[pl.ds(0, 7)], dst.at[pl.ds(0, 7)], s, r, device_id=z_peer(1)[1], device_id_type=MESH
        )
        sent.append(seven)

        def wait():
            seven.wait_recv()
            own.wait()

        return wait

    def exchange_o(src_at, dst_at, some):
        s, r, l = new_sem(), new_sem(), new_sem()
        own = pltpu.make_async_copy(src_at(o), dst_at(o), l)
        for dx, dy, dc in FAR_FIRST:
            other, device = near(dx, dy, dc)
            pltpu.make_async_remote_copy(
                src_at(other), dst_at(o), s, r, device_id=device, device_id_type=MESH
            ).start()
        own.start()
        rest = pltpu.make_async_remote_copy(
            some, some, s, r, device_id=near(0, 0, 1)[1], device_id_type=MESH
        )
        sent.append(rest)

        def wait():
            rest.wait_recv()
            own.wait()

        return wait

    def rows_at(ref, q):
        return lambda k: ref.at[q, k // 16, :, pl.ds(pl.multiple_of(k % 16 * 8, 8), 8), :]

    def planes_at(ref, q):
        return lambda k: ref.at[q, :, k // 4, :, pl.ds(pl.multiple_of(k % 4 * 128, 128), 128)]

    wait_a, wait_b, wait_c, wait_d = {}, {}, {}, {}

    def there(q):
        wait_a[q]()

        def of(lo, first, rows):
            return jnp.concatenate([ra[q, 2 * h + lo, first : first + rows] for h in range(4)], 0)

        even, odd = of(0, 0, 32), of(1, 0, 32)
        sb[q, 0, 0] = (even + odd).T
        sb[q, 1, 0] = (even - odd).T
        even, odd = of(0, 32, 16), of(1, 32, 16)
        turned = jnp.concatenate([even + odd, even - odd], 0).T
        sb[q, 0, 1] = turned
        sb[q, 1, 1] = turned
        wait_b[q] = exchange_o(rows_at(sb, q), planes_at(rb, q), other_way.at[q])

    def middle(q):
        wait_b[q]()
        if q == 0:
            for name in ("whole", "fermi0", "fermi1", "bose0", "bose1", "mirror"):
                loads[name].wait()
        both = jnp.concatenate([rb[q, 0].reshape(64, 512), rb[q, 1].reshape(64, 512)], 1)
        lattice = table_by_data(whole, both)
        g = in_time(data_by_table(lattice[:, :512], fermi[0], fermi[1]), True)
        v1r, v1i, v2r, v2i = in_time(data_by_table(lattice[:, 512:], bose[0], bose[1]), False)
        g1r, g1i, g2r, g2i = g
        same = jnp.where(jnp.logical_and(z == 0, o % 16 == 0), 1, 0) if q < 2 else 0
        turn = mirror[same][:, :32]
        high, low = split(jnp.concatenate(g, 1))
        turned = dot(turn, high) + dot(turn, low)
        m1r, m1i, m2r, m2i = [turned[:, 256 * k : 256 * k + 256] for k in range(4)]
        b1r, b1i = g1i * m2i - g1r * m2r, -(g1r * m2i + g1i * m2r)
        b2r, b2i = g2i * m1i - g2r * m1r, -(g2r * m1i + g2i * m1r)
        s1r, s1i = v1r * g1r - v1i * g1i, v1r * g1i + v1i * g1r
        s2r, s2i = v2r * g2r - v2i * g2i, v2r * g2i + v2i * g2r
        if q == 0:
            for name in ("fermib0", "fermib1", "boseb0", "boseb1", "wholeb"):
                loads[name].wait()
        omega = data_by_table(
            out_of_time(s1r - s2r, s1i - s2i, s1r + s2r, s1i + s2i), fermib[0], fermib[1]
        )
        nu = data_by_table(out_of_time(b1r + b2r, b1i + b2i, b1r - b2r, b1i - b2i), boseb[0], boseb[1])
        planes = table_by_data(wholeb, jnp.concatenate([omega, nu], 1))
        tb[q, 0] = planes[:, :512].reshape(8, 8, 512)
        tb[q, 1] = planes[:, 512:].reshape(8, 8, 512)
        wait_c[q] = exchange_o(planes_at(tb, q), rows_at(ub, q), other_way.at[q])

    def back(q):
        wait_c[q]()
        even, odd = ub[q, 0, 0].T, ub[q, 1, 0].T
        both = (ub[q, 0, 1] + ub[q, 1, 1]).T
        for lo in range(2):
            fermi_rows = even - odd if lo else even + odd
            bose_rows = both[:64] - both[64:] if lo else both[:64] + both[64:]
            for h in range(4):
                ta[q, 2 * h + lo, :32] = fermi_rows[32 * h : 32 * h + 32]
                ta[q, 2 * h + lo, 32:] = bose_rows[16 * h : 16 * h + 16]
        wait_d[q] = exchange_z(ta.at[q], ua.at[q])

    other_way = sb.reshape(4, 64, 8, 128).at[:, pl.ds(0, 62)]

    for name in ("x_g0", "x_g1", "x_v0", "x_v1"):
        loads[name].wait()
    sheet_there(x_g, x_v, sheet, loads, sa)
    pl.semaphore_wait(barrier, 38)
    for q in range(4):
        wait_a[q] = exchange_z(sa.at[q], ra.at[q])

    load("whole", whole_h.at[parity], whole)
    load("mirror", mirror_h.at[parity], mirror)
    for k in range(2):
        load("fermi" + str(k), fermi_h.at[k], fermi.at[k])
        load("bose" + str(k), bose_h.at[parity, k], bose.at[k])
    load("wholeb", wholeb_h.at[parity], wholeb)
    for k in range(2):
        load("fermib" + str(k), fermib_h.at[k], fermib.at[k])
        load("boseb" + str(k), boseb_h.at[parity, k], boseb.at[k])
    for k in range(2):
        load("sheetb" + str(k), sheetb_h.at[pl.ds(4 * k, 4)], sheetb.at[pl.ds(4 * k, 4)])

    there(0)
    there(1)
    middle(0)
    there(2)
    middle(1)
    back(0)
    there(3)
    middle(2)
    back(1)
    middle(3)
    back(2)
    back(3)

    loads["sheetb0"].wait()
    loads["sheetb1"].wait()
    wait_d[0]()
    wait_d[1]()
    for k, term in enumerate(sheet_back(ua, 0, sheetb)):
        half[k] = term
    wait_d[2]()
    wait_d[3]()
    terms = [half[k] + term for k, term in enumerate(sheet_back(ua, 1, sheetb))]
    re, im = eight([t[:, :128] for t in terms], [t[:, 128:] for t in terms], -1)
    for p, part in enumerate((re, im)):
        for g in range(8):
            for b in range(2):
                y_g[p, pl.ds(2 * g + b, 32, 16), :] = part[g][48 * b : 48 * b + 32]
                y_v[p, pl.ds(2 * g + b, 16, 16), :] = part[g][48 * b + 32 : 48 * b + 48]
    puts = []
    for p in range(2):
        for h in range(2):
            rows = pl.ds(256 * h, 256)
            puts.append(pltpu.make_async_copy(y_g.at[p, rows], out_g.at[p, rows], put_sem.at[len(puts)]))
        puts.append(pltpu.make_async_copy(y_v.at[p], out_v.at[p], put_sem.at[len(puts)]))
    for put in puts:
        put.start()
    for copy in sent:
        copy.wait_send()
    for put in puts:
        put.wait()


def hand_on(g, v, out_g, out_v, held_g, held_v, sem):
    ways = []
    for p in range(2):
        for half in range(2):
            ways.append([r.at[p, pl.ds(256 * half, 256)] for r in (g, held_g, out_g)])
        ways.append([r.at[p] for r in (v, held_v, out_v)])
    first = [pltpu.make_async_copy(a, b, sem.at[k]) for k, (a, b, _) in enumerate(ways)]
    second = [pltpu.make_async_copy(b, c, sem.at[6 + k]) for k, (_, b, c) in enumerate(ways)]
    for copy in first:
        copy.start()
    for there, back in zip(first, second):
        there.wait()
        back.start()
    for copy in second:
        copy.wait()


def view(x):
    n = x.shape[-3]
    return x.reshape(2, n, 2, 8, 128).transpose(0, 1, 3, 2, 4).reshape(2, n * 16, 128)


def unview(x):
    n = x.shape[1] // 16
    return x.reshape(2, n, 8, 2, 128).transpose(0, 1, 3, 2, 4).reshape(2, n, 2, 1024)


def per_device(green, inter):
    shapes = [
        (2, 512, 128), (2, 256, 128),
        (8, 2, 256, 256), (8, 2, 256, 256), (2, 64, 128), (2, 64, 128),
        (2, 512, 512), (2, 512, 512), (2, 512, 512), (2, 512, 512), (2, 32, 128),
        (4, 8, 48, 128), (4, 8, 48, 128), (4, 2, 2, 128, 128), (4, 2, 8, 8, 512),
        (4, 2, 8, 8, 512), (4, 2, 2, 128, 128), (4, 8, 48, 128), (4, 8, 48, 128),
        (8, 96, 256), (2, 512, 128), (2, 256, 128),
    ]
    scratch = [pltpu.VMEM(s, BF16 if 2 <= k < 11 else F32) for k, s in enumerate(shapes)]
    any_spec = pl.BlockSpec(memory_space=pl.ANY)
    constants = tables()
    out_g, out_v = pl.pallas_call(
        kernel,
        out_shape=(
            jax.ShapeDtypeStruct((2, 512, 128), F32),
            jax.ShapeDtypeStruct((2, 256, 128), F32),
        ),
        in_specs=[any_spec] * (2 + len(constants)),
        out_specs=(any_spec, any_spec),
        scratch_shapes=scratch + [pltpu.SemaphoreType.DMA((n,)) for n in (26, 6, 48)],
        compiler_params=pltpu.CompilerParams(
            collective_id=0, has_side_effects=True, vmem_limit_bytes=56 << 20
        ),
    )(view(green), view(inter), *constants)
    out_g, out_v = pl.pallas_call(
        hand_on,
        out_shape=(jax.ShapeDtypeStruct((2, 512, 128), F32), jax.ShapeDtypeStruct((2, 256, 128), F32)),
        in_specs=[any_spec] * 2,
        out_specs=(any_spec, any_spec),
        scratch_shapes=[
            pltpu.VMEM((2, 512, 128), F32),
            pltpu.VMEM((2, 256, 128), F32),
            pltpu.SemaphoreType.DMA((12,)),
        ],
    )(out_g, out_v)
    return unview(out_g), unview(out_v)[None]


def solution(mesh):
    placed = (P(None, None, "freq", "kz", None), P(None, None, "freq", "kz", None))
    return jax.shard_map(
        per_device,
        mesh=mesh,
        in_specs=placed,
        out_specs=(P(None, "freq", "kz", None), P(None, None, "freq", "kz", None)),
        check_vma=False,
    )
```

time: 63.3 us -> 57.1 us (0.902)
  Pallas kernels: 62.6 us -> 56 us
    pallas_call x1, Pallas kernels: 60.6 us -> 54.1 us  [per_device(): pl.pallas_call(kernel, out_shape=(jax.ShapeDtypeStruct((2, 512, 128), F32...]
where the time goes in v3:
time: 57.1 us; the launch traced here: 56.7 us
  Pallas kernels  56 us (98%)
  between operations  0.64 us (1%)
    pallas_call x1, Pallas kernels, per_device(): pl.pallas_call(kernel, out_shape=(jax.ShapeDtypeStruct((2, 512, 128), F32...  54.1 us
    pallas_call x1, Pallas kernels, per_device(): pl.pallas_call(hand_on, out_shape=(jax.ShapeDtypeStruct((2, 512, 128), F3...  1.97 us

profile of v3, /device:TPU:1, one launch (start us, length us, event | category | flops | bytes accessed | tf_op | source)
XLA Modules:
  0.0 56.7 jit_solution(16773785726074541756)
XLA Ops:
  0.6 54.1 %shard_map.122 = (f32[2,512,128]{2,1,0:T(8,128)}, f32[2,256,128]{2,1,0:T(8,128)}) custom-call(f32[2,512,128]{2,1,0:T(8,128)} %bitcast.20, f32[2,256,128]{2,1,0:T(8,128)} %bitcast.21, bf16[8,2,256,256]{3,2,1,0:T(8,128)(2,1)} %constant.18.clone.sheet_h, bf16[8,2,256,256]{3,2,1,0:T(8,128)(2,1)} %constant.19.clone.sheetb_h, ...), custom_call_target="tpu_custom_call" | custom-call | tf_op jit(solution)/shard_map/pallas_call | solution.py:526
  54.7 2.0 %shard_map.123 = (f32[2,512,128]{2,1,0:T(8,128)}, f32[2,256,128]{2,1,0:T(8,128)}) custom-call(f32[2,512,128]{2,1,0:T(8,128)} %get-tuple-element.6.g, f32[2,256,128]{2,1,0:T(8,128)} %get-tuple-element.7.v), custom_call_target="tpu_custom_call" | custom-call | tf_op jit(solution)/shard_map/pallas_call | solution.py:539

commit v4 on v3

--- a/solution.py
+++ b/solution.py
@@ -271,7 +271,7 @@
     green, inter, sheet_h, sheetb_h, whole_h, wholeb_h, fermi_h, fermib_h, bose_h, boseb_h, mirror_h,
     out_g, out_v,
     x_g, x_v, sheet, sheetb, whole, wholeb, fermi, fermib, bose, boseb, mirror,
-    sa, ra, sb, rb, tb, ub, ta, ua, half, y_g, y_v, load_sem, put_sem, sem,
+    sa, ra, sb, rb, tb, ub, ta, ua, half, load_sem, sem,
 ):
     kz, freq = lax.axis_index("kz"), lax.axis_index("freq")
     z_lo, c = kz // 8, kz % 8
@@ -468,36 +468,22 @@
     for p, part in enumerate((re, im)):
         for g in range(8):
             for b in range(2):
-                y_g[p, pl.ds(2 * g + b, 32, 16), :] = part[g][48 * b : 48 * b + 32]
-                y_v[p, pl.ds(2 * g + b, 16, 16), :] = part[g][48 * b + 32 : 48 * b + 48]
-    puts = []
-    for p in range(2):
-        for h in range(2):
-            rows = pl.ds(256 * h, 256)
-            puts.append(pltpu.make_async_copy(y_g.at[p, rows], out_g.at[p, rows], put_sem.at[len(puts)]))
-        puts.append(pltpu.make_async_copy(y_v.at[p], out_v.at[p], put_sem.at[len(puts)]))
-    for put in puts:
-        put.start()
+                out_g[p, pl.ds(2 * g + b, 32, 16), :] = part[g][48 * b : 48 * b + 32]
+                out_v[p, pl.ds(2 * g + b, 16, 16), :] = part[g][48 * b + 32 : 48 * b + 48]
     for copy in sent:
         copy.wait_send()
-    for put in puts:
-        put.wait()
-
-
-def hand_on(g, v, out_g, out_v, held_g, held_v, sem):
+
+
+def hand_on(g, v, out_g, out_v, sem):
     ways = []
     for p in range(2):
         for half in range(2):
-            ways.append([r.at[p, pl.ds(256 * half, 256)] for r in (g, held_g, out_g)])
-        ways.append([r.at[p] for r in (v, held_v, out_v)])
-    first = [pltpu.make_async_copy(a, b, sem.at[k]) for k, (a, b, _) in enumerate(ways)]
-    second = [pltpu.make_async_copy(b, c, sem.at[6 + k]) for k, (_, b, c) in enumerate(ways)]
-    for copy in first:
+            ways.append([r.at[p, pl.ds(256 * half, 256)] for r in (g, out_g)])
+        ways.append([r.at[p] for r in (v, out_v)])
+    copies = [pltpu.make_async_copy(a, b, sem.at[k]) for k, (a, b) in enumerate(ways)]
+    for copy in copies:
         copy.start()
-    for there, back in zip(first, second):
-        there.wait()
-        back.start()
-    for copy in second:
+    for copy in copies:
         copy.wait()
 
 
@@ -518,20 +504,18 @@
         (2, 512, 512), (2, 512, 512), (2, 512, 512), (2, 512, 512), (2, 32, 128),
         (4, 8, 48, 128), (4, 8, 48, 128), (4, 2, 2, 128, 128), (4, 2, 8, 8, 512),
         (4, 2, 8, 8, 512), (4, 2, 2, 128, 128), (4, 8, 48, 128), (4, 8, 48, 128),
-        (8, 96, 256), (2, 512, 128), (2, 256, 128),
+        (8, 96, 256),
     ]
     scratch = [pltpu.VMEM(s, BF16 if 2 <= k < 11 else F32) for k, s in enumerate(shapes)]
     any_spec = pl.BlockSpec(memory_space=pl.ANY)
+    vmem_spec = pl.BlockSpec(memory_space=pltpu.VMEM)
     constants = tables()
     out_g, out_v = pl.pallas_call(
         kernel,
-        out_shape=(
-            jax.ShapeDtypeStruct((2, 512, 128), F32),
-            jax.ShapeDtypeStruct((2, 256, 128), F32),
-        ),
+        out_shape=(pltpu.VMEM((2, 512, 128), F32), pltpu.VMEM((2, 256, 128), F32)),
         in_specs=[any_spec] * (2 + len(constants)),
-        out_specs=(any_spec, any_spec),
-        scratch_shapes=scratch + [pltpu.SemaphoreType.DMA((n,)) for n in (26, 6, 48)],
+        out_specs=(vmem_spec, vmem_spec),
+        scratch_shapes=scratch + [pltpu.SemaphoreType.DMA((n,)) for n in (26, 48)],
         compiler_params=pltpu.CompilerParams(
             collective_id=0, has_side_effects=True, vmem_limit_bytes=56 << 20
         ),
@@ -539,14 +523,10 @@
     out_g, out_v = pl.pallas_call(
         hand_on,
         out_shape=(jax.ShapeDtypeStruct((2, 512, 128), F32), jax.ShapeDtypeStruct((2, 256, 128), F32)),
-        in_specs=[any_spec] * 2,
+        in_specs=[vmem_spec] * 2,
         out_specs=(any_spec, any_spec),
-        scratch_shapes=[
-            pltpu.VMEM((2, 512, 128), F32),
-            pltpu.VMEM((2, 256, 128), F32),
-            pltpu.SemaphoreType.DMA((12,)),
-        ],
-    )(out_g, out_v)
+        scratch_shapes=[pltpu.SemaphoreType.DMA((6,))],
+    )(*[pltpu.with_memory_space_constraint(x, pltpu.VMEM) for x in (out_g, out_v)])
     return unview(out_g), unview(out_v)[None]
 
 

time: 57.1 us -> 55.1 us (0.965)
  Pallas kernels: 56 us -> 54.1 us
    pallas_call x1, Pallas kernels: 1.97 us -> 0.93 us  [per_device(): pl.pallas_call(hand_on, out_shape=(jax.ShapeDtypeStruct((2, 512, 128), F3...]
    pallas_call x1, Pallas kernels: 54.1 us -> 53.2 us  [per_device(): pl.pallas_call(kernel, out_shape=(pltpu.VMEM((2, 512, 128), F32), pltpu.V...]
where the time goes in v4:
time: 55.1 us; the launch traced here: 54.8 us
  Pallas kernels  54.1 us (98%)
  between operations  0.64 us (1%)
    pallas_call x1, Pallas kernels, per_device(): pl.pallas_call(kernel, out_shape=(pltpu.VMEM((2, 512, 128), F32), pltpu.V...  53.2 us

profile of v4, /device:TPU:1, one launch (start us, length us, event | category | flops | bytes accessed | tf_op | source)
XLA Modules:
  0.0 54.8 jit_solution(7994209192680031899)
XLA Ops:
  0.6 53.2 %shard_map.122 = (f32[2,512,128]{2,1,0:T(8,128)S(1)}, f32[2,256,128]{2,1,0:T(8,128)S(1)}) custom-call(f32[2,512,128]{2,1,0:T(8,128)} %bitcast.20, f32[2,256,128]{2,1,0:T(8,128)} %bitcast.21, bf16[8,2,256,256]{3,2,1,0:T(8,128)(2,1)} %constant.18.clone.sheet_h, bf16[8,2,256,256]{3,2,1,0:T(8,128)(2,1)} %constant.19.clone.sheetb_h, ...), custom_call_target="tpu_custom_call" | custom-call | tf_op jit(solution)/shard_map/pallas_call | solution.py:513
  53.8 0.9 %shard_map.123 = (f32[2,512,128]{2,1,0:T(8,128)}, f32[2,256,128]{2,1,0:T(8,128)}) custom-call(f32[2,512,128]{2,1,0:T(8,128)S(1)} %get-tuple-element.6.g, f32[2,256,128]{2,1,0:T(8,128)S(1)} %get-tuple-element.7.v), custom_call_target="tpu_custom_call" | custom-call | tf_op jit(solution)/shard_map/pallas_call | solution.py:523

commit v5 on v4

--- a/solution.py
+++ b/solution.py
@@ -55,31 +55,36 @@
     xl = np.repeat(np.arange(4), 32)
     ky = np.tile(np.arange(32), 4)
     for residue in range(8):
-        site = columns(residue).reshape(2, 2, 16, 2, 2).transpose(0, 2, 1, 3, 4)
+        site = columns(residue).reshape(2, 2, 16, 2, 2).transpose(0, 1, 3, 2, 4)
         x, y = site[..., 0], site[..., 1]
         assert (x % 8 == residue).all()
         turns = xl[:, None, None, None, None] * x + ky[:, None, None, None, None] * y
         angle = 2 * np.pi * (turns % 32) / 32
         c, s = np.cos(angle) / 32, np.sin(angle) / 32
-        real = np.stack([c, s], 4)
-        imag = np.stack([-s, c], 4)
+        real = np.stack([c, s], 3)
+        imag = np.stack([-s, c], 3)
         tables.append(np.concatenate([real, imag], 0).reshape(256, 256))
     return np.stack(tables)
 
 
 def depth_tables():
-    whole = np.zeros((2, 2, 16, 2, 16, 2, 2))
+    whole = np.zeros((2, 96, 96))
     kappa = np.arange(16)
+    depth = np.arange(16)
     for parity in range(2):
-        depth = 2 * np.arange(16) + parity
-        angle = 2 * np.pi * ((depth[:, None] * kappa) % 32) / 32
+        angle = 2 * np.pi * (((2 * depth[:, None] + parity) * kappa) % 32) / 32
         c, s = np.cos(angle) / math.sqrt(32), np.sin(angle) / math.sqrt(32)
-        for e in range(2):
-            whole[parity, 0, :, e, :, 0, e] = c
-            whole[parity, 0, :, e, :, 1, e] = -s
-            whole[parity, 1, :, e, :, 0, e] = s
-            whole[parity, 1, :, e, :, 1, e] = c
-    return whole.reshape(2, 64, 64)
+        parts = [[c, -s], [s, c]]
+        for new in range(2):
+            for old in range(2):
+                for b in range(2):
+                    block = parts[new][old][:, b::2]
+                    for e in range(2):
+                        row = new * 32 + e * 16
+                        whole[parity, row : row + 16, b * 4 + old * 2 + e :: 12] = block
+                    row = 64 + new * 16
+                    whole[parity, row : row + 16, 8 + b * 2 + old :: 12] = block
+    return whole
 
 
 def angles(length, offset):
@@ -94,11 +99,8 @@
 
 
 def bose_table():
-    theta = angles(256, 0).reshape(4, 4, 16, 256).transpose(1, 0, 2, 3)
-    table = np.zeros((2, 4, 2, 4, 16, 512))
-    for parity in range(2):
-        table[parity, :, parity] = np.concatenate([np.cos(theta), np.sin(theta)], -1)
-    return table.reshape(2, 512, 512)
+    theta = angles(256, 0).reshape(4, 4, 16, 256).transpose(1, 0, 2, 3).reshape(256, 256)
+    return np.concatenate([np.cos(theta), np.sin(theta)], 1)
 
 
 def mirror_tables():
@@ -108,7 +110,8 @@
             for depth in range(16):
                 other = (-depth - parity) % 16
                 for e in range(2):
-                    tables[parity, same, 2 * depth + e, 2 * other + (e if same else 1 - e)] = 1
+                    f = e if same else 1 - e
+                    tables[parity, same, 16 * e + depth, 16 * f + other] = 1
     return tables.astype(ml_dtypes.bfloat16)
 
 
@@ -132,8 +135,8 @@
         by_parity(whole.transpose(0, 2, 1)),
         split_table(fermi),
         split_table(fermi.T),
-        by_parity(bose / 16),
-        by_parity(bose.transpose(0, 2, 1) / math.sqrt(512)),
+        split_table(bose / 16),
+        split_table(bose.T / math.sqrt(512)),
         mirror_tables(),
     )
 
@@ -208,8 +211,8 @@
         )
 
     yr, yi = eight([rows(0, g) for g in range(8)], [rows(1, g) for g in range(8)], 1)
-    first = lane(96, 256) % 2 == 0
-    plane = lane(48, 128) % 8 < 4
+    first = lane(96, 256) // 16 % 2 == 0
+    plane = lane(48, 128) < 64
 
     def one(residue):
         loads["sheet" + str(residue)].wait()
@@ -220,8 +223,8 @@
         for high in range(2):
             zero = value[:48, 128 * high : 128 * high + 128]
             one_ = value[48:, 128 * high : 128 * high + 128]
-            out[2 * high, group] = jnp.where(plane, zero, pltpu.roll(one_, 4, 1))
-            out[2 * high + 1, group] = jnp.where(plane, pltpu.roll(zero, 124, 1), one_)
+            out[2 * high, group] = jnp.where(plane, zero, pltpu.roll(one_, 64, 1))
+            out[2 * high + 1, group] = jnp.where(plane, pltpu.roll(zero, 64, 1), one_)
 
     put(0, one(0))
     put(1, one(4))
@@ -232,15 +235,15 @@
 
 
 def sheet_back(x, high, table):
-    first = lane(96, 128) % 2 == 0
-    plane = lane(48, 128) % 8 < 4
+    first = lane(96, 128) // 16 % 2 == 0
+    plane = lane(48, 128) < 64
 
     def get(group):
         a, b = x[2 * high, group], x[2 * high + 1, group]
         return jnp.concatenate(
             [
-                jnp.where(plane, a, pltpu.roll(b, 4, 1)),
-                jnp.where(plane, pltpu.roll(a, 124, 1), b),
+                jnp.where(plane, a, pltpu.roll(b, 64, 1)),
+                jnp.where(plane, pltpu.roll(a, 64, 1), b),
             ],
             0,
         )
@@ -253,6 +256,27 @@
         held[n] = jnp.where(first, b, a)
     part = pl.ds(128 * high, 128)
     return [data_by_table(held[k], table[k, 0, part, :], table[k, 1, part, :]) for k in range(8)]
+
+
+def apart(x):
+    rows, columns = x.shape
+    lower = lane(rows, 128) < 64
+    ones, twos = [], []
+    for k in range(0, columns, 256):
+        a, b = x[:, k : k + 128], x[:, k + 128 : k + 256]
+        ones.append(jnp.where(lower, a, pltpu.roll(b, 64, 1)))
+        twos.append(jnp.where(lower, pltpu.roll(a, 64, 1), b))
+    return jnp.concatenate(ones, 1), jnp.concatenate(twos, 1)
+
+
+def together(ones, twos):
+    lower = lane(ones.shape[0], 128) < 64
+    pieces = []
+    for k in range(0, ones.shape[1], 128):
+        a, b = ones[:, k : k + 128], twos[:, k : k + 128]
+        pieces.append(jnp.where(lower, a, pltpu.roll(b, 64, 1)))
+        pieces.append(jnp.where(lower, pltpu.roll(a, 64, 1), b))
+    return jnp.concatenate(pieces, 1)
 
 
 def in_time(p, odd):
@@ -356,10 +380,10 @@
         return wait
 
     def rows_at(ref, q):
-        return lambda k: ref.at[q, k // 16, :, pl.ds(pl.multiple_of(k % 16 * 8, 8), 8), :]
+        return lambda k: ref.at[q, k // 16, pl.ds(pl.multiple_of(k % 16 * 12, 4), 12), :]
 
     def planes_at(ref, q):
-        return lambda k: ref.at[q, :, k // 4, :, pl.ds(pl.multiple_of(k % 4 * 128, 128), 128)]
+        return lambda k: ref.at[q, k % 4, pl.ds(pl.multiple_of(k // 4 * 12, 4), 12), :]
 
     wait_a, wait_b, wait_c, wait_d = {}, {}, {}, {}
 
@@ -370,23 +394,27 @@
             return jnp.concatenate([ra[q, 2 * h + lo, first : first + rows] for h in range(4)], 0)
 
         even, odd = of(0, 0, 32), of(1, 0, 32)
-        sb[q, 0, 0] = (even + odd).T
-        sb[q, 1, 0] = (even - odd).T
+        for k, value in enumerate(((even + odd).T, (even - odd).T)):
+            for r in range(8):
+                sb[q, k, pl.ds(r, 16, 12), :] = value[16 * r : 16 * r + 16]
         even, odd = of(0, 32, 16), of(1, 32, 16)
-        turned = jnp.concatenate([even + odd, even - odd], 0).T
-        sb[q, 0, 1] = turned
-        sb[q, 1, 1] = turned
-        wait_b[q] = exchange_o(rows_at(sb, q), planes_at(rb, q), other_way.at[q])
+        value = jnp.concatenate([even + odd, even - odd], 0).T
+        for r in range(4):
+            one, two = value[32 * r : 32 * r + 16], value[32 * r + 16 : 32 * r + 32]
+            sb[q, 0, pl.ds(8 + r, 16, 12), :] = jnp.where(lower, one, pltpu.roll(two, 64, 1))
+            sb[q, 1, pl.ds(8 + r, 16, 12), :] = jnp.where(lower, pltpu.roll(one, 64, 1), two)
+        wait_b[q] = exchange_o(rows_at(sb, q), planes_at(rb, q), other_way)
 
     def middle(q):
         wait_b[q]()
         if q == 0:
             for name in ("whole", "fermi0", "fermi1", "bose0", "bose1", "mirror"):
                 loads[name].wait()
-        both = jnp.concatenate([rb[q, 0].reshape(64, 512), rb[q, 1].reshape(64, 512)], 1)
-        lattice = table_by_data(whole, both)
-        g = in_time(data_by_table(lattice[:, :512], fermi[0], fermi[1]), True)
-        v1r, v1i, v2r, v2i = in_time(data_by_table(lattice[:, 512:], bose[0], bose[1]), False)
+        lattice = table_by_data(whole, jnp.concatenate([rb[q, k] for k in range(4)], 1))
+        g = in_time(data_by_table(lattice[:64], fermi[0], fermi[1]), True)
+        one, two = apart(lattice[64:])
+        v = jnp.concatenate([one[:16], two[:16], one[16:], two[16:]], 0)
+        v1r, v1i, v2r, v2i = in_time(data_by_table(v, bose[0], bose[1]), False)
         g1r, g1i, g2r, g2i = g
         same = jnp.where(jnp.logical_and(z == 0, o % 16 == 0), 1, 0) if q < 2 else 0
         turn = mirror[same][:, :32]
@@ -404,15 +432,25 @@
             out_of_time(s1r - s2r, s1i - s2i, s1r + s2r, s1i + s2i), fermib[0], fermib[1]
         )
         nu = data_by_table(out_of_time(b1r + b2r, b1i + b2i, b1r - b2r, b1i - b2i), boseb[0], boseb[1])
-        planes = table_by_data(wholeb, jnp.concatenate([omega, nu], 1))
-        tb[q, 0] = planes[:, :512].reshape(8, 8, 512)
-        tb[q, 1] = planes[:, 512:].reshape(8, 8, 512)
-        wait_c[q] = exchange_o(planes_at(tb, q), rows_at(ub, q), other_way.at[q])
+        nu = together(
+            jnp.concatenate([nu[:16], nu[32:48]], 0), jnp.concatenate([nu[16:32], nu[48:]], 0)
+        )
+        planes = table_by_data(wholeb, jnp.concatenate([omega, nu], 0))
+        for k in range(4):
+            tb[q, k] = planes[:, 128 * k : 128 * k + 128]
+        wait_c[q] = exchange_o(planes_at(tb, q), rows_at(ub, q), other_way)
 
     def back(q):
         wait_c[q]()
-        even, odd = ub[q, 0, 0].T, ub[q, 1, 0].T
-        both = (ub[q, 0, 1] + ub[q, 1, 1]).T
+        even, odd = [
+            jnp.concatenate([ub[q, k, pl.ds(r, 16, 12), :] for r in range(8)], 0).T for k in range(2)
+        ]
+        pieces = []
+        for r in range(4):
+            one, two = [ub[q, k, pl.ds(8 + r, 16, 12), :] for k in range(2)]
+            pieces.append(jnp.where(lower, one, pltpu.roll(two, 64, 1)))
+            pieces.append(jnp.where(lower, pltpu.roll(one, 64, 1), two))
+        both = jnp.concatenate(pieces, 0).T
         for lo in range(2):
             fermi_rows = even - odd if lo else even + odd
             bose_rows = both[:64] - both[64:] if lo else both[:64] + both[64:]
@@ -421,7 +459,8 @@
                 ta[q, 2 * h + lo, 32:] = bose_rows[16 * h : 16 * h + 16]
         wait_d[q] = exchange_z(ta.at[q], ua.at[q])
 
-    other_way = sb.reshape(4, 64, 8, 128).at[:, pl.ds(0, 62)]
+    other_way = x_g.at[0, pl.ds(0, 372)]
+    lower = lane(16, 128) < 64
 
     for name in ("x_g0", "x_g1", "x_v0", "x_v1"):
         loads[name].wait()
@@ -434,11 +473,11 @@
     load("mirror", mirror_h.at[parity], mirror)
     for k in range(2):
         load("fermi" + str(k), fermi_h.at[k], fermi.at[k])
-        load("bose" + str(k), bose_h.at[parity, k], bose.at[k])
+        load("bose" + str(k), bose_h.at[k], bose.at[k])
     load("wholeb", wholeb_h.at[parity], wholeb)
     for k in range(2):
         load("fermib" + str(k), fermib_h.at[k], fermib.at[k])
-        load("boseb" + str(k), boseb_h.at[parity, k], boseb.at[k])
+        load("boseb" + str(k), boseb_h.at[k], boseb.at[k])
     for k in range(2):
         load("sheetb" + str(k), sheetb_h.at[pl.ds(4 * k, 4)], sheetb.at[pl.ds(4 * k, 4)])
 
@@ -500,10 +539,10 @@
 def per_device(green, inter):
     shapes = [
         (2, 512, 128), (2, 256, 128),
-        (8, 2, 256, 256), (8, 2, 256, 256), (2, 64, 128), (2, 64, 128),
-        (2, 512, 512), (2, 512, 512), (2, 512, 512), (2, 512, 512), (2, 32, 128),
-        (4, 8, 48, 128), (4, 8, 48, 128), (4, 2, 2, 128, 128), (4, 2, 8, 8, 512),
-        (4, 2, 8, 8, 512), (4, 2, 2, 128, 128), (4, 8, 48, 128), (4, 8, 48, 128),
+        (8, 2, 256, 256), (8, 2, 256, 256), (2, 96, 128), (2, 96, 128),
+        (2, 512, 512), (2, 512, 512), (2, 256, 512), (2, 512, 256), (2, 32, 128),
+        (4, 8, 48, 128), (4, 8, 48, 128), (4, 2, 192, 128), (4, 4, 96, 128),
+        (4, 4, 96, 128), (4, 2, 192, 128), (4, 8, 48, 128), (4, 8, 48, 128),
         (8, 96, 256),
     ]
     scratch = [pltpu.VMEM(s, BF16 if 2 <= k < 11 else F32) for k, s in enumerate(shapes)]

time: 55.1 us -> 52.5 us (0.953)
  Pallas kernels: 54.1 us -> 51.7 us
    pallas_call x1, Pallas kernels: 53.2 us -> 50.8 us  [per_device(): pl.pallas_call(kernel, out_shape=(pltpu.VMEM((2, 512, 128), F32), pltpu.V...]
where the time goes in v5:
time: 52.5 us; the launch traced here: 52.4 us
  Pallas kernels  51.7 us (98%)
  between operations  0.64 us (1%)
    pallas_call x1, Pallas kernels, per_device(): pl.pallas_call(kernel, out_shape=(pltpu.VMEM((2, 512, 128), F32), pltpu.V...  50.8 us

profile of v5, /device:TPU:1, one launch (start us, length us, event | category | flops | bytes accessed | tf_op | source)
XLA Modules:
  0.0 52.4 jit_solution(6248975356234299322)
XLA Ops:
  0.6 50.8 %shard_map.122 = (f32[2,512,128]{2,1,0:T(8,128)S(1)}, f32[2,256,128]{2,1,0:T(8,128)S(1)}) custom-call(f32[2,512,128]{2,1,0:T(8,128)} %bitcast.20, f32[2,256,128]{2,1,0:T(8,128)} %bitcast.21, bf16[8,2,256,256]{3,2,1,0:T(8,128)(2,1)} %constant.18.clone.sheet_h, bf16[8,2,256,256]{3,2,1,0:T(8,128)(2,1)} %constant.19.clone.sheetb_h, ...), custom_call_target="tpu_custom_call" | custom-call | tf_op jit(solution)/shard_map/pallas_call | solution.py:552
  51.5 0.9 %shard_map.123 = (f32[2,512,128]{2,1,0:T(8,128)}, f32[2,256,128]{2,1,0:T(8,128)}) custom-call(f32[2,512,128]{2,1,0:T(8,128)S(1)} %get-tuple-element.6.g, f32[2,256,128]{2,1,0:T(8,128)S(1)} %get-tuple-element.7.v), custom_call_target="tpu_custom_call" | custom-call | tf_op jit(solution)/shard_map/pallas_call | solution.py:562

commit v6 on v5

--- a/solution.py
+++ b/solution.py
@@ -486,8 +486,8 @@
     middle(0)
     there(2)
     middle(1)
+    there(3)
     back(0)
-    there(3)
     middle(2)
     back(1)
     middle(3)
@@ -501,6 +501,8 @@
     for k, term in enumerate(sheet_back(ua, 0, sheetb)):
         half[k] = term
     wait_d[2]()
+    for copy in sent:
+        copy.wait_send()
     wait_d[3]()
     terms = [half[k] + term for k, term in enumerate(sheet_back(ua, 1, sheetb))]
     re, im = eight([t[:, :128] for t in terms], [t[:, 128:] for t in terms], -1)
@@ -509,8 +511,6 @@
             for b in range(2):
                 out_g[p, pl.ds(2 * g + b, 32, 16), :] = part[g][48 * b : 48 * b + 32]
                 out_v[p, pl.ds(2 * g + b, 16, 16), :] = part[g][48 * b + 32 : 48 * b + 48]
-    for copy in sent:
-        copy.wait_send()
 
 
 def hand_on(g, v, out_g, out_v, sem):

time: 52.5 us -> 52.4 us (level)
  no operation moved by 1% of the time
where the time goes in v6:
time: 52.4 us; the launch traced here: 52.3 us
  Pallas kernels  51.6 us (98%)
  between operations  0.64 us (1%)
    pallas_call x1, Pallas kernels, per_device(): pl.pallas_call(kernel, out_shape=(pltpu.VMEM((2, 512, 128), F32), pltpu.V...  50.7 us

profile of v6, /device:TPU:1, one launch (start us, length us, event | category | flops | bytes accessed | tf_op | source)
XLA Modules:
  0.0 52.3 jit_solution(256085154145278794)
XLA Ops:
  0.6 50.7 %shard_map.122 = (f32[2,512,128]{2,1,0:T(8,128)S(1)}, f32[2,256,128]{2,1,0:T(8,128)S(1)}) custom-call(f32[2,512,128]{2,1,0:T(8,128)} %bitcast.20, f32[2,256,128]{2,1,0:T(8,128)} %bitcast.21, bf16[8,2,256,256]{3,2,1,0:T(8,128)(2,1)} %constant.18.clone.sheet_h, bf16[8,2,256,256]{3,2,1,0:T(8,128)(2,1)} %constant.19.clone.sheetb_h, ...), custom_call_target="tpu_custom_call" | custom-call | tf_op jit(solution)/shard_map/pallas_call | solution.py:552
  51.3 0.9 %shard_map.123 = (f32[2,512,128]{2,1,0:T(8,128)}, f32[2,256,128]{2,1,0:T(8,128)}) custom-call(f32[2,512,128]{2,1,0:T(8,128)S(1)} %get-tuple-element.6.g, f32[2,256,128]{2,1,0:T(8,128)S(1)} %get-tuple-element.7.v), custom_call_target="tpu_custom_call" | custom-call | tf_op jit(solution)/shard_map/pallas_call | solution.py:562
